TPU v7x, 256 devices: a whole 4x4x8 slice. The times are simulated.
256 devices in a mesh: rows: 16 (over x, z_lo), cols: 16 (over z_hi, y, core).
Axes of the slice: x: 4, y: 4, z: 8 (z_hi: 2, z_lo: 4; z = z_hi * 4 + z_lo), core: 2. Of those that a mesh axis runs over, the one named last changes fastest.
Arguments:
- matrix: bfloat16 [16384, 65536], P('rows', 'cols'), may hold values from -0.0234375 to 0.0234375
- cost_pred: bfloat16 [64, 65536], P(None, 'cols'), may hold values from -800 to 800
- cost_true: bfloat16 [64, 65536], P(None, 'cols'), may hold values from -1200 to 1200
- dual_start: float32 [64, 16384], P(None, 'rows'), may hold values from -3 to 3
- right_side: float32 [16384], P('rows'), may hold values from -3 to 3
- bound_code: int32 [65536], P('cols'), may hold values from 0 to 3
- step_numer: int32 [64, 3], replicated, may hold values from 2 to 9
- step_denom: int32 [64, 3], replicated, may hold values from 10 to 17
Outputs:
- primal_end: float32 [64, 65536], P(None, 'cols')
- dual_end: float32 [64, 16384], P(None, 'rows')
- cost_grad: float32 [64, 65536], P(None, 'cols')
All inputs are finite; a program needn't handle non-finite values.
Results may differ from a plain program's by a relative error of at most 0.0017.
Values may be sent and summed in bfloat16 or wider, within the bound.
A program may use at most 64 MiB of HBM per device.

v0:
```python
import jax
import jax.numpy as jnp
from jax import lax
from jax.sharding import PartitionSpec as P

VARS = 65536
ITERS = 2


sharpness = 16.0
eps_norm = 1e-06


def smooth_slope(shifted, lower_bound, upper_bound):
    return jax.nn.sigmoid(sharpness * (shifted - lower_bound)) * jax.nn.sigmoid(
        sharpness * (upper_bound - shifted)
    )


def bounds_of(bound_code):
    low_bit = (bound_code % 2).astype(jnp.float32)
    high_bit = (bound_code // 2).astype(jnp.float32)
    return (-0.25 - 0.75 * low_bit, 0.25 + 0.75 * high_bit)


def matrix_times(primal_bf, matrix):
    return lax.dot_general(
        primal_bf, matrix, (((1,), (1,)), ((), ())), preferred_element_type=jnp.float32
    )


def local(matrix, cost_pred, cost_true, dual_start, right_side, bound_code, step_numer, step_denom):
    instances = cost_pred.shape[0]
    primal_weight = (lax.axis_index("rows") == 0).astype(jnp.float32)
    dual_weight = (lax.axis_index("cols") == 0).astype(jnp.float32)
    costs_all = cost_pred.astype(jnp.float32)
    norm_sum = lax.psum(jnp.sum(costs_all * costs_all, axis=1, keepdims=True), "cols")
    scale_all = jnp.sqrt(norm_sum / VARS + eps_norm)
    ratios = step_numer.astype(jnp.float32) / step_denom.astype(jnp.float32)
    tau_all = ratios[:, 0:1] / scale_all
    sigma_all = ratios[:, 1:2] * scale_all
    truth = cost_true.astype(jnp.float32)
    theta_step = ratios[:, 2:3]
    lower_bound, upper_bound = bounds_of(bound_code)

    def dual_image(dual_full):
        return lax.psum(jnp.dot(dual_full, matrix, preferred_element_type=jnp.float32), "rows")

    def primal_image(primal_bf):
        return lax.psum(matrix_times(primal_bf, matrix), "cols")

    primal = jnp.zeros_like(costs_all)
    dual_state = dual_start
    dual_full = dual_start.astype(jnp.bfloat16)
    history = []
    for turn in range(ITERS):
        if turn > 0:
            dual_full = dual_state.astype(jnp.bfloat16)
        reduced = costs_all - dual_image(dual_full)
        shifted = primal - tau_all * reduced
        projected = jnp.clip(shifted, lower_bound, upper_bound)
        extended = projected + theta_step * (projected - primal)
        residue = right_side[None, :] - primal_image(extended.astype(jnp.bfloat16))
        dual_state = dual_state + sigma_all * residue
        history.append((reduced, shifted, residue))
        primal = projected
    adjoint_primal = truth
    adjoint_dual = None
    gradient = jnp.zeros_like(costs_all)
    factors = jnp.zeros((instances, 1), jnp.float32)
    for turn in reversed(range(ITERS)):
        reduced, shifted, residue = history[turn]
        carried = jnp.zeros_like(costs_all)
        forward_adj = adjoint_primal
        if adjoint_dual is not None:
            sigma_part = sigma_all * jnp.sum(adjoint_dual * residue, axis=1, keepdims=True)
            sigma_term = sigma_part * dual_weight
            factors = factors + lax.psum(sigma_term, ("rows", "cols"))
            backward_adj = -sigma_all * dual_image(adjoint_dual.astype(jnp.bfloat16))
            forward_adj = adjoint_primal + (1.0 + theta_step) * backward_adj
            carried = -theta_step * backward_adj
        slope_adj = smooth_slope(shifted, lower_bound, upper_bound) * forward_adj
        tau_part = tau_all * jnp.sum(slope_adj * reduced, axis=1, keepdims=True)
        tau_term = tau_part * primal_weight
        factors = factors + lax.psum(tau_term, ("rows", "cols"))
        gradient = gradient - tau_all * slope_adj
        adjoint_primal = slope_adj + carried
        if turn > 0:
            pushed = primal_image((tau_all * slope_adj).astype(jnp.bfloat16))
            adjoint_dual = pushed
    gradient = gradient + costs_all * factors / (VARS * scale_all * scale_all)
    return (primal, dual_state, gradient)


def solution(mesh):
    placed = (
        P("rows", "cols"),
        P(None, "cols"),
        P(None, "cols"),
        P(None, "rows"),
        P("rows"),
        P("cols"),
        P(),
        P(),
    )
    return jax.shard_map(
        local,
        mesh=mesh,
        in_specs=placed,
        out_specs=(P(None, "cols"), P(None, "rows"), P(None, "cols")),
        check_vma=False,
    )
```

profile of v0, /device:TPU:1, one launch (start us, length us, event | category | flops | bytes accessed | tf_op | source)
XLA Modules:
  0.0 990.0 jit_solution(14065277587993927152)
XLA Ops:
  7.2 0.0 copy-start
  7.2 0.0 copy-start.9
  7.2 0.0 copy-start.10
  7.2 0.0 copy-start.8
  7.2 0.0 all-reduce.7.cloned.1.call-start
  7.3 6.1 fusion.23
  13.3 0.0 copy-start.2
  13.3 0.0 copy-start.7
  13.3 0.0 all-reduce.7.cloned.1.call-update
  13.3 0.0 all-reduce.9.cloned.1.call-start
  13.4 0.0 copy-done
  13.4 0.2 fusion.1
  13.6 45.7 %psum.70 = f32[64,1]{0,1:T(1,128)S(1)} all-reduce(f32[64,1]{0,1:T(1,128)S(1)} %bitcast.47), channel_id=1, replica_groups=mesh['rows'=16,'cols'=16] {'cols'}, use_global_device_ids=true, to_apply=%region_1.0 | all-reduce | flops 64 | bytes 512 | tf_op jit(solution)/shard_map/psum | solution.py:37
  59.3 0.0 copy-done.9
  59.3 0.0 copy-done.10
  59.3 0.0 copy-done.8
  59.4 113.3 %all-reduce.7.cloned.1.call-done = f32[64,4096]{1,0:T(8,128)} async-done(((f32[64,4096]{1,0:T(8,128)}), f32[64,4096]{1,0:T(8,128)}) %all-reduce.7.cloned.1.call-update) | async-done | bytes 1048592 | tf_op jit(solution)/shard_map/psum | solution.py:47
  172.7 7.1 fusion.6
  179.8 0.0 all-reduce.9.cloned.1.call-update
  179.8 0.0 all-reduce.11.cloned.1.call-start
  179.9 184.6 %all-reduce.9.cloned.1.call-done = f32[64,1024]{1,0:T(8,128)} async-done(((f32[64,1024]{1,0:T(8,128)}), f32[64,1024]{1,0:T(8,128)}) %all-reduce.9.cloned.1.call-update) | async-done | bytes 262160 | tf_op jit(solution)/shard_map/psum | solution.py:50
  364.5 0.0 copy-done.2
  364.5 0.0 copy-done.7
  364.5 0.0 copy-start.1
  364.5 0.0 copy-start.6
  364.5 6.2 fusion.21
  370.7 0.0 all-reduce.11.cloned.1.call-update
  370.7 0.0 all-reduce.15.cloned.1.call-start
  370.8 156.3 %all-reduce.11.cloned.1.call-done = f32[64,4096]{1,0:T(8,128)} async-done(((f32[64,4096]{1,0:T(8,128)}), f32[64,4096]{1,0:T(8,128)}) %all-reduce.11.cloned.1.call-update) | async-done | bytes 1048592 | tf_op jit(solution)/shard_map/psum | solution.py:47
  527.1 0.0 copy-done.1
  527.1 0.0 copy-done.6
  527.1 2.2 convert_multiply_fusion.2
  529.3 0.0 copy-start.3
  529.3 7.1 fusion.4
  536.4 0.0 copy-done.3
  536.4 6.8 fusion.5
  543.2 0.0 all-reduce.15.cloned.1.call-update
  543.2 0.2 all-reduce.13.cloned.1.call-start
  543.5 185.8 %all-reduce.15.cloned.1.call-done = (f32[64,1024]{1,0:T(8,128)}, f32[64,1024]{1,0:T(8,128)}) async-done(((f32[64,1024]{1,0:T(8,128)}, f32[64,1024]{1,0:T(8,128)}), (f32[64,1024]{1,0:T(8,128)}, f32[64,1024]{1,0:T(8,128)})) %all-reduce.15.cloned.1.call-update) | async-done | bytes 524304 | tf_op jit(solution)/shard_map/psum | solution.py:50
  729.3 6.1 fusion.19
  735.4 0.0 all-reduce.13.cloned.1.call-update
  735.4 0.0 copy-done.4
  735.4 0.0 copy-done.5
  735.4 1.9 multiply_reduce_fusion.2
  737.3 154.7 %all-reduce.13.cloned.1.call-done = f32[64,4096]{1,0:T(8,128)} async-done(((f32[64,4096]{1,0:T(8,128)}), f32[64,4096]{1,0:T(8,128)}) %all-reduce.13.cloned.1.call-update) | async-done | bytes 1048592 | tf_op jit(solution)/shard_map/psum | solution.py:47
  892.0 3.6 multiply_reduce_fusion.1
  895.6 85.3 %psum.81 = f32[64,1]{0,1:T(1,128)S(1)} all-reduce(f32[64,1]{0,1:T(1,128)S(1)} %fusion.35), channel_id=1, replica_groups=mesh['rows'=16,'cols'=16] {'rows','cols'}, use_global_device_ids=true, to_apply=%region_9.10 | all-reduce | flops 64 | bytes 512 | tf_op jit(solution)/shard_map/psum | solution.py:85
  980.9 2.5 fusion.3
  (6 shorter events, 0.1 us)
Async XLA Ops:
  7.2 6.2 copy-start
  7.2 52.1 %copy-start.9 = (s32[64,3]{0,1:T(4,128)S(1)}, s32[64,3]{0,1:T(4,128)}, u32[]{:S(2)}) copy-start(s32[64,3]{0,1:T(4,128)} %param.15) | copy-start | bytes 2308
  7.2 52.1 %copy-start.10 = (s32[64,3]{0,1:T(4,128)S(1)}, s32[64,3]{0,1:T(4,128)}, u32[]{:S(2)}) copy-start(s32[64,3]{0,1:T(4,128)} %param.14) | copy-start | bytes 2308
  7.2 52.1 %copy-start.8 = (s32[4096]{0:T(1024)S(1)}, s32[4096]{0:T(1024)}, u32[]{:S(2)}) copy-start(s32[4096]{0:T(1024)} %param.13) | copy-start | bytes 49156
  7.2 165.5 %all-reduce.7.cloned.1.call-start = ((), (), s32[]{:S(2)}) async-start(), calls=%async_computation | async-start | bytes 2097152 | tf_op jit(solution)/shard_map/psum | solution.py:47
  13.3 351.2 %copy-start.2 = (f32[64,1024]{1,0:T(8,128)S(1)}, f32[64,1024]{1,0:T(8,128)}, u32[]{:S(2)}) copy-start(f32[64,1024]{1,0:T(8,128)} %param.11) | copy-start | bytes 786436
  13.3 351.2 %copy-start.7 = (f32[1024]{0:T(1024)S(1)}, f32[1024]{0:T(1024)}, u32[]{:S(2)}) copy-start(f32[1024]{0:T(1024)} %param.12) | copy-start | bytes 12292
  13.3 351.2 %all-reduce.9.cloned.1.call-start = ((), (), s32[]{:S(2)}) async-start(), calls=%async_computation.1 | async-start | bytes 524288 | tf_op jit(solution)/shard_map/psum | solution.py:50
  179.8 347.3 %all-reduce.11.cloned.1.call-start = ((), (), s32[]{:S(2)}) async-start(), calls=%async_computation.2 | async-start | bytes 2097152 | tf_op jit(solution)/shard_map/psum | solution.py:47
  364.5 162.6 %copy-start.1 = (f32[64,4096]{1,0:T(8,128)S(1)}, f32[64,4096]{1,0:T(8,128)}, u32[]{:S(2)}) copy-start(f32[64,4096]{1,0:T(8,128)} %all-reduce.7.cloned.1.call-done) | copy-start | bytes 3145732
  364.5 162.6 %copy-start.6 = (bf16[64,4096]{1,0:T(8,128)(2,1)S(1)}, bf16[64,4096]{1,0:T(8,128)(2,1)}, u32[]{:S(2)}) copy-start(bf16[64,4096]{1,0:T(8,128)(2,1)} %param.10) | copy-start | bytes 1572868
  370.7 358.5 %all-reduce.15.cloned.1.call-start = ((), (), s32[]{:S(2)}) async-start(), calls=%async_computation.4 | async-start | bytes 1048576 | tf_op jit(solution)/shard_map/psum | solution.py:50
  529.3 7.2 copy-start.3
  543.2 348.8 %all-reduce.13.cloned.1.call-start = ((), (), s32[]{:S(2)}) async-start(), calls=%async_computation.3 | async-start | bytes 2097152 | tf_op jit(solution)/shard_map/psum | solution.py:47
  729.3 6.1 copy-start.4
  729.3 6.1 copy-start.5
Sparse Core Ops, SparseCore 0:
  13.5 159.1 all-reduce.6
  179.9 184.5 all-reduce.8
  370.9 156.1 all-reduce.10
  543.3 185.8 all-reduce.14
  735.5 156.4 all-reduce.12
where the time goes:
time: 990 us
  waiting for transfers between devices  795 us (80%)
  blocking collectives  131 us (13%)
  matrix products  39.3 us (4%)
  between operations  13.9 us (1%)
  other arithmetic  10.4 us (1%)
    psum x3, waiting for transfers between devices, dual_image(): lax.psum(jnp.dot(dual_full, matrix, preferred_element_type=jnp.float32),...  424 us
    psum x2, waiting for transfers between devices, primal_image(): return lax.psum(matrix_times(primal_bf, matrix), 'cols')  370 us
    psum x1, blocking collectives, local(): factors = factors + lax.psum(tau_term, ('rows', 'cols'))  85.3 us
    psum x1, blocking collectives, local(): lax.psum(jnp.sum(costs_all * costs_all, axis=1, keepdims=True), 'cols')  45.7 us
    dot_general x3, matrix products, matrix_times(): lax.dot_general(primal_bf, matrix, (((1,), (1,)), ((), ())), preferred_el...  21 us
  transfers between devices with their start and end apart: 5, of which 5 were waited for; matrix products, arithmetic and copies ran while one was open for 0% of the time, Pallas kernels for 0%

commit v1 on v0

v1 whole, which is shorter than its diff:
```python
import jax
import jax.numpy as jnp
from jax import lax
from jax.experimental import pallas as pl
from jax.experimental.pallas import tpu as pltpu
from jax.sharding import PartitionSpec as P

VARS = 65536
MESH = pl.DeviceIdType.MESH
F32 = jnp.float32
BF16 = jnp.bfloat16
SHARP = 16.0
EPS = 1e-06

INST = 64
HALF = 32
ROWS = 1024
COLS = 4096
SIDE = 4
WIDE = COLS // SIDE
CHUNK = WIDE // SIDE
TEAM = 8
PIECE = ROWS // TEAM
LANES = 128


def kernel(
    m_hbm, cp_ref, ct_ref, d0_ref, right_ref, code_ref, numer_ref, denom_ref,
    primal_ref, dual_ref, grad_ref,
    m_ref, m_sem,
    tau_ref, sigma_ref, theta_ref, scale2_ref, low_ref, high_ref, sum_ref,
    dbf_ref, own0_ref, own1_ref, t0_ref, t1_ref, red0_ref, sh0_ref, slope0_ref, sa1_ref, e_ref, z_ref,
    s1x, s1z, r1x, r1z, s2z, s2x, r2z, r2x, gather,
    a_ss, a_rs, f_ss, f_rs,
    sb, rb, zs, zr, gb, gd,
    b_ss, b_rs, z_ss, z_rs, g_ss, g_rs, gd_ss, gd_rs,
    rows_t, rows_p, rows_pr, rowx, rowz,
    t_ss, t_rs, p_ss, p_rs, rx_ss, rx_rs, rz_ss, rz_rs,
    dual1_ref, weigh_ref, wimg_ref,
):
    rr = lax.axis_index("rows")
    cc = lax.axis_index("cols")
    x, zl = rr // SIDE, lax.rem(rr, SIDE)
    zh, yc = cc // TEAM, lax.rem(cc, TEAM)
    y, core = yc // 2, lax.rem(yc, 2)

    def around(value, step, size):
        return lax.rem(value + step + size, size)

    def x_peer(k):
        return (around(x, k, SIDE) * SIDE + zl, cc)

    def z_peer(k):
        return (x * SIDE + around(zl, k, SIDE), cc)

    def team_peer(k):
        return (rr, zh * TEAM + around(yc, k, TEAM))

    far_peer = (rr, (1 - zh) * TEAM + yc)

    def remote(src, dst, send, recv, peer):
        copy = pltpu.make_async_remote_copy(
            src_ref=src, dst_ref=dst, send_sem=send, recv_sem=recv, device_id=peer, device_id_type=MESH
        )
        copy.start()
        return copy

    def at(value, size):
        return pl.ds(pl.multiple_of(value * size, size), size)

    order = (2, 1, 3, 0)
    loads = []
    for k in order:
        cols = at(around(x, k, SIDE), WIDE)
        load = pltpu.make_async_copy(m_hbm.at[:, cols], m_ref.at[:, cols], m_sem.at[k])
        load.start()
        loads.append(load)

    barrier = pltpu.get_barrier_semaphore()
    for k in (1, 2, 3):
        pl.semaphore_signal(barrier, inc=1, device_id=x_peer(k), device_id_type=MESH)
        pl.semaphore_signal(barrier, inc=1, device_id=z_peer(k), device_id_type=MESH)
    for k in range(1, TEAM):
        pl.semaphore_signal(barrier, inc=1, device_id=team_peer(k), device_id_type=MESH)
    pl.semaphore_signal(barrier, inc=1, device_id=far_peer, device_id_type=MESH)

    lane = lax.broadcasted_iota(jnp.int32, (INST, LANES), 1)
    diagonal = lane == lax.broadcasted_iota(jnp.int32, (INST, LANES), 0)

    def to_row(column):
        spread = jnp.where(diagonal, jnp.broadcast_to(column, (INST, LANES)), 0.0)
        return jnp.broadcast_to(jnp.sum(spread, axis=0, keepdims=True), (8, LANES))

    def to_column(row):
        spread = jnp.where(diagonal, jnp.broadcast_to(row[0:1, :], (INST, LANES)), 0.0)
        return jnp.sum(spread, axis=1, keepdims=True)

    sum_ref[...] = jnp.zeros_like(sum_ref)

    def square_step(i, _):
        c = cp_ref[:, at(i, LANES)].astype(F32)
        sum_ref[...] += c * c
        return 0

    lax.fori_loop(0, COLS // LANES, square_step, 0, unroll=4)
    squares = jnp.sum(sum_ref[...], axis=1, keepdims=True)
    rows_t[0, yc] = to_row(squares)

    dbf_ref[...] = d0_ref[...].astype(BF16)
    code = code_ref[...]
    half_code = code // 2
    low_ref[...] = -0.25 - 0.75 * (code - 2 * half_code).astype(F32)
    high_ref[...] = 0.25 + 0.75 * half_code.astype(F32)
    theta_ref[...] = jnp.broadcast_to(numer_ref[:, 2:3].astype(F32) / denom_ref[:, 2:3].astype(F32), (INST, LANES))

    pl.semaphore_wait(barrier, 14)

    def team_rows(which):
        return [
            remote(rows_t.at[which, yc], rows_t.at[which, yc], t_ss.at[which, k - 1], t_rs.at[which, k - 1], team_peer(k))
            for k in range(1, TEAM)
        ]

    def wait_all(copies):
        for c in copies:
            c.wait()

    def sum_team(which):
        total = rows_t[which, 0]
        for i in range(1, TEAM):
            total = total + rows_t[which, i]
        return total

    def far_row(which):
        return remote(rows_p.at[which], rows_pr.at[which], p_ss.at[which], p_rs.at[which], far_peer)

    norm_copies = team_rows(0)

    def scatter_dual(first):
        sends = []
        for position, k in enumerate(order):
            j = around(x, k, SIDE)
            if first:
                loads[position].wait()
            out = jnp.dot(dbf_ref[...], m_ref[:, at(j, WIDE)], preferred_element_type=F32)
            if k:
                s1x[k - 1] = out[:HALF].astype(BF16)
                sends.append(remote(s1x.at[k - 1], r1x.at[k - 1], a_ss.at[0, k - 1], a_rs.at[0, k - 1], x_peer(k)))
            else:
                own0_ref[...] = out[:HALF]
            own1_ref[j] = out[HALF:]
        for k in (2, 1, 3):
            cols = at(around(zl, k, SIDE), CHUNK)
            s1z[k - 1] = own1_ref[:, :, cols].astype(BF16)
            sends.append(remote(s1z.at[k - 1], r1z.at[k - 1], a_ss.at[1, k - 1], a_rs.at[1, k - 1], z_peer(k)))
        return sends

    def second_dual(sends):
        later = []
        for c in sends[:3]:
            c.wait()
        t0_ref[...] = own0_ref[...] + r1x[0].astype(F32) + r1x[1].astype(F32) + r1x[2].astype(F32)
        for k in (2, 1, 3):
            s2z[k - 1] = t0_ref[:, at(around(zl, k, SIDE), CHUNK)].astype(BF16)
            later.append(remote(s2z.at[k - 1], r2z.at[k - 1], a_ss.at[2, k - 1], a_rs.at[2, k - 1], z_peer(k)))
        for c in sends[3:]:
            c.wait()
        t1_ref[...] = own1_ref[:, :, at(zl, CHUNK)] + r1z[0].astype(F32) + r1z[1].astype(F32) + r1z[2].astype(F32)
        for k in (2, 1, 3):
            s2x[k - 1] = t1_ref[around(x, k, SIDE)].astype(BF16)
            later.append(remote(s2x.at[k - 1], r2x.at[k - 1], a_ss.at[3, k - 1], a_rs.at[3, k - 1], x_peer(k)))
        return later

    def gather_dual(later):
        wait_all(later)
        upper = t0_ref[:, at(zl, CHUNK)] + r2z[0].astype(F32) + r2z[1].astype(F32) + r2z[2].astype(F32)
        lower = t1_ref[x] + r2x[0].astype(F32) + r2x[1].astype(F32) + r2x[2].astype(F32)
        gather[x, zl, :HALF] = upper.astype(BF16)
        gather[x, zl, HALF:] = lower.astype(BF16)
        mine = gather.at[x, zl]
        z_own = {}
        x_own = {}
        for k in (1, 3, 2):
            z_own[k] = remote(mine, mine, a_ss.at[4, k - 1], a_rs.at[4, k - 1], z_peer(k))
            x_own[k] = remote(mine, mine, a_ss.at[5, k - 1], a_rs.at[5, k - 1], x_peer(k))
        forwards = []
        for k in (1, 3, 2):
            z_own[k].wait()
            part = gather.at[x, around(zl, -k, SIDE), pl.ds(0, HALF)]
            for q in (1, 3, 2):
                forwards.append(remote(part, part, f_ss.at[0, k - 1, q - 1], f_rs.at[0, k - 1, q - 1], x_peer(q)))
            x_own[k].wait()
            part = gather.at[around(x, -k, SIDE), zl, pl.ds(HALF, HALF)]
            for q in (1, 3, 2):
                forwards.append(remote(part, part, f_ss.at[1, k - 1, q - 1], f_rs.at[1, k - 1, q - 1], z_peer(q)))
        wait_all(forwards)

    def each_piece(body):
        def step(i, _):
            gx = i // (SIDE * 2)
            gz = lax.rem(i // 2, SIDE)
            part = lax.rem(i, 2)
            body(gx, gz, at(part, LANES), at(i, LANES))
            return 0

        lax.fori_loop(0, COLS // LANES, step, 0, unroll=2)

    def primal_images(use, lhs_rows, lhs_uses):
        sends = []
        for k in (2, 1, 3, 0):
            yk = around(y, k, SIDE)
            out = lax.dot_general(
                e_ref[lhs_rows, :], m_ref[at(yk, 2 * PIECE), :], (((1,), (1,)), ((), ())), preferred_element_type=F32
            )
            for n, u in enumerate(lhs_uses):
                z_ref[u, yk * 2] = out[n * INST : (n + 1) * INST, :PIECE]
                z_ref[u, yk * 2 + 1] = out[n * INST : (n + 1) * INST, PIECE:]

    def scatter_primal(u):
        sends = []
        for k in (4, 5, 3, 2, 6, 1, 7):
            sb[u, k - 1] = z_ref[u, around(yc, k, TEAM)].astype(BF16)
            sends.append(remote(sb.at[u, k - 1], rb.at[u, k - 1], b_ss.at[u, k - 1], b_rs.at[u, k - 1], team_peer(k)))
        return sends

    def far_primal(u, sends):
        wait_all(sends)
        total = z_ref[u, yc]
        for k in range(1, TEAM):
            total = total + rb[u, k - 1].astype(F32)
        zs[u] = total.astype(BF16)
        return remote(zs.at[u], zr.at[u], z_ss.at[u], z_rs.at[u], far_peer)

    def done_primal(u, copy):
        copy.wait()
        return zs[u].astype(F32) + zr[u].astype(F32)

    def gather_primal(v):
        return [
            remote(gb.at[v, yc], gb.at[v, yc], g_ss.at[v, k - 1], g_rs.at[v, k - 1], team_peer(k))
            for k in (4, 5, 3, 2, 6, 1, 7)
        ]

    def fill_dual(v):
        for i in range(TEAM):
            dbf_ref[:, i * PIECE : (i + 1) * PIECE] = gb[v, i]

    own_cols = at(yc, PIECE)

    sends = scatter_dual(True)
    wait_all(norm_copies)
    rows_p[0] = sum_team(0)
    norm_far = far_row(0)
    later = second_dual(sends)
    norm_far.wait()
    norm_sum = to_column(rows_p[0] + rows_pr[0])
    scale = jnp.sqrt(norm_sum / VARS + EPS)
    tau_ref[...] = jnp.broadcast_to(numer_ref[:, 0:1].astype(F32) / denom_ref[:, 0:1].astype(F32) / scale, (INST, LANES))
    sigma_ref[...] = jnp.broadcast_to(numer_ref[:, 1:2].astype(F32) / denom_ref[:, 1:2].astype(F32) * scale, (INST, LANES))
    scale2_ref[...] = jnp.broadcast_to(VARS * scale * scale, (INST, LANES))
    gather_dual(later)

    def first_step(gx, gz, lanes, cols):
        image = gather[gx, gz, :, lanes].astype(F32)
        reduced = cp_ref[:, cols].astype(F32) - image
        shifted = 0.0 - tau_ref[...] * reduced
        projected = jnp.minimum(jnp.maximum(shifted, low_ref[:, cols]), high_ref[:, cols])
        red0_ref[:, cols] = reduced
        sh0_ref[:, cols] = shifted
        e_ref[:INST, cols] = (projected + theta_ref[...] * projected).astype(BF16)

    each_piece(first_step)

    primal_images(0, slice(0, INST), (0,))
    sends = scatter_primal(0)

    def slope_of(shifted, cols):
        return jax.nn.sigmoid(SHARP * (shifted - low_ref[:, cols])) * jax.nn.sigmoid(
            SHARP * (high_ref[:, cols] - shifted)
        )

    def slope_step(gx, gz, lanes, cols):
        slope = slope_of(sh0_ref[:, cols], cols)
        slope0_ref[:, cols] = slope
        e_ref[INST:, cols] = (slope * red0_ref[:, cols]).astype(BF16)

    each_piece(slope_step)
    primal_images(1, slice(INST, 2 * INST), (1,))
    far = far_primal(0, sends)
    weigh_sends = scatter_primal(1)
    image = done_primal(0, far)
    residue0 = right_ref[:, own_cols] - image
    dual1 = d0_ref[:, own_cols] + sigma_ref[...] * residue0
    dual1_ref[...] = dual1
    weigh_ref[...] = sigma_ref[...] * residue0
    gb[0, yc] = dual1.astype(BF16)
    wait_all(gather_primal(0))
    fill_dual(0)

    sends = scatter_dual(False)
    weigh_far = far_primal(1, weigh_sends)
    later = second_dual(sends)
    wimg_ref[...] = (
        tau_ref[...] * (1.0 + theta_ref[...]) * sigma_ref[...] * done_primal(1, weigh_far)
    )
    gather_dual(later)
    sum_ref[...] = jnp.zeros_like(sum_ref)

    def second_step(gx, gz, lanes, cols):
        image = gather[gx, gz, :, lanes].astype(F32)
        low, high = low_ref[:, cols], high_ref[:, cols]
        reduced = cp_ref[:, cols].astype(F32) - image
        before = jnp.minimum(jnp.maximum(sh0_ref[:, cols], low), high)
        shifted = before - tau_ref[...] * reduced
        projected = jnp.minimum(jnp.maximum(shifted, low), high)
        primal_ref[:, cols] = projected
        e_ref[INST:, cols] = (projected + theta_ref[...] * (projected - before)).astype(BF16)
        slope_adj = slope_of(shifted, cols) * ct_ref[:, cols].astype(F32)
        sa1_ref[:, cols] = slope_adj
        e_ref[:INST, cols] = (tau_ref[...] * slope_adj).astype(BF16)
        sum_ref[...] += slope_adj * reduced + slope_adj * (slope0_ref[:, cols] * red0_ref[:, cols])

    each_piece(second_step)
    rows_t[1, yc] = to_row(tau_ref[:, 0:1] * jnp.sum(sum_ref[...], axis=1, keepdims=True))

    primal_images(2, slice(0, 2 * INST), (2, 3))
    sends = scatter_primal(2)
    factor_copies = team_rows(1)
    far = far_primal(2, sends)
    end_sends = scatter_primal(3)
    wait_all(factor_copies)
    rows_p[1] = sum_team(1)
    factor_far = far_row(1)
    adjoint = done_primal(2, far)
    rounded = adjoint.astype(BF16)
    gb[1, yc] = rounded
    gathers = gather_primal(1)
    weighed = adjoint * weigh_ref[...] - rounded.astype(F32) * wimg_ref[...]
    rows_t[2, yc] = to_row(jnp.sum(weighed, axis=1, keepdims=True))
    factor_copies = team_rows(2)
    wait_all(gathers)
    fill_dual(1)

    sends = scatter_dual(False)
    end_far = far_primal(3, end_sends)
    wait_all(factor_copies)
    rowx[x] = sum_team(2)
    x_rows = [remote(rowx.at[x], rowx.at[x], rx_ss.at[k - 1], rx_rs.at[k - 1], x_peer(k)) for k in (1, 2, 3)]
    later = second_dual(sends)
    wait_all(x_rows)
    rowz[zl] = rowx[0] + rowx[1] + rowx[2] + rowx[3]
    z_rows = [remote(rowz.at[zl], rowz.at[zl], rz_ss.at[k - 1], rz_rs.at[k - 1], z_peer(k)) for k in (1, 2, 3)]
    factor_far.wait()
    residue1 = right_ref[:, own_cols] - done_primal(3, end_far)
    gd[yc] = dual1_ref[...] + sigma_ref[...] * residue1
    dual_gathers = [
        remote(gd.at[yc], gd.at[yc], gd_ss.at[k - 1], gd_rs.at[k - 1], team_peer(k)) for k in (4, 5, 3, 2, 6, 1, 7)
    ]
    gather_dual(later)
    wait_all(z_rows)
    factors = to_column(rows_p[1] + rows_pr[1] + (rowz[0] + rowz[1] + rowz[2] + rowz[3]))
    sum_ref[...] = jnp.broadcast_to(factors, (INST, LANES)) / scale2_ref[...]

    def last_step(gx, gz, lanes, cols):
        image = gather[gx, gz, :, lanes].astype(F32)
        slope_adj = sa1_ref[:, cols]
        ahead = slope_adj - (1.0 + theta_ref[...]) * (sigma_ref[...] * image)
        gradient = tau_ref[...] * (slope_adj + slope0_ref[:, cols] * ahead)
        grad_ref[:, cols] = cp_ref[:, cols].astype(F32) * sum_ref[...] - gradient

    each_piece(last_step)
    wait_all(dual_gathers)
    for i in range(TEAM):
        dual_ref[:, i * PIECE : (i + 1) * PIECE] = gd[i]


def local(matrix, cost_pred, cost_true, dual_start, right_side, bound_code, step_numer, step_denom):
    dma = pltpu.SemaphoreType.DMA
    v = pltpu.VMEM
    whole = pl.BlockSpec(memory_space=pltpu.VMEM)
    uses, rows = 4, 3
    scratch = [
        v((ROWS, COLS), BF16), dma((SIDE,)),
        v((INST, LANES), F32), v((INST, LANES), F32), v((INST, LANES), F32), v((INST, LANES), F32),
        v((1, COLS), F32), v((1, COLS), F32), v((INST, LANES), F32),
        v((INST, ROWS), BF16), v((HALF, WIDE), F32), v((SIDE, HALF, WIDE), F32), v((HALF, WIDE), F32),
        v((SIDE, HALF, CHUNK), F32), v((INST, COLS), F32), v((INST, COLS), F32), v((INST, COLS), F32),
        v((INST, COLS), F32), v((2 * INST, COLS), BF16), v((uses, TEAM, INST, PIECE), F32),
        v((3, HALF, WIDE), BF16), v((3, SIDE, HALF, CHUNK), BF16), v((3, HALF, WIDE), BF16), v((3, SIDE, HALF, CHUNK), BF16),
        v((3, HALF, CHUNK), BF16), v((3, HALF, CHUNK), BF16), v((3, HALF, CHUNK), BF16), v((3, HALF, CHUNK), BF16),
        v((SIDE, SIDE, INST, CHUNK), BF16),
        dma((6, 3)), dma((6, 3)), dma((2, 3, 3)), dma((2, 3, 3)),
        v((uses, TEAM - 1, INST, PIECE), BF16), v((uses, TEAM - 1, INST, PIECE), BF16),
        v((uses, INST, PIECE), BF16), v((uses, INST, PIECE), BF16),
        v((2, TEAM, INST, PIECE), BF16), v((TEAM, INST, PIECE), F32),
        dma((uses, TEAM - 1)), dma((uses, TEAM - 1)), dma((uses,)), dma((uses,)),
        dma((2, TEAM - 1)), dma((2, TEAM - 1)), dma((TEAM - 1,)), dma((TEAM - 1,)),
        v((rows, TEAM, 8, LANES), F32), v((2, 8, LANES), F32), v((2, 8, LANES), F32), v((SIDE, 8, LANES), F32),
        v((SIDE, 8, LANES), F32),
        dma((rows, TEAM - 1)), dma((rows, TEAM - 1)), dma((2,)), dma((2,)), dma((3,)), dma((3,)), dma((3,)), dma((3,)),
        v((INST, PIECE), F32), v((INST, PIECE), F32), v((INST, PIECE), F32),
    ]
    return pl.pallas_call(
        kernel,
        out_shape=(
            jax.ShapeDtypeStruct((INST, COLS), F32),
            jax.ShapeDtypeStruct((INST, ROWS), F32),
            jax.ShapeDtypeStruct((INST, COLS), F32),
        ),
        in_specs=[pl.BlockSpec(memory_space=pl.ANY)] + [whole] * 7,
        out_specs=(whole, whole, whole),
        scratch_shapes=scratch,
        compiler_params=pltpu.CompilerParams(
            collective_id=0, has_side_effects=True, vmem_limit_bytes=52 * 2**20
        ),
    )(
        matrix,
        cost_pred,
        cost_true,
        dual_start,
        right_side.reshape(1, ROWS),
        bound_code.reshape(1, COLS),
        step_numer,
        step_denom,
    )


def solution(mesh):
    placed = (
        P("rows", "cols"),
        P(None, "cols"),
        P(None, "cols"),
        P(None, "rows"),
        P("rows"),
        P("cols"),
        P(),
        P(),
    )
    return jax.shard_map(
        local,
        mesh=mesh,
        in_specs=placed,
        out_specs=(P(None, "cols"), P(None, "rows"), P(None, "cols")),
        check_vma=False,
    )
```

time: 990 us -> 129 us (0.13)
  waiting for transfers between devices: 795 us -> 0 us
  blocking collectives: 131 us -> 0 us
  Pallas kernels: 0 us -> 115 us
  matrix products: 39.3 us -> 0 us
  between operations: 13.9 us -> 0.65 us
  local copies, waits for them, and re-layouts: 0.05 us -> 11.2 us
  other arithmetic: 10.4 us -> 0 us
    psum x5 -> x0, waiting for transfers between devices: 795 us -> none  [the longest x3 424 us: dual_image(): lax.psum(jnp.dot(dual_full, matrix, preferred_element_type=jnp.float32),...]
    psum x2 -> x0, blocking collectives: 131 us -> none  [the longest x1 85.3 us: local(): factors = factors + lax.psum(tau_term, ('rows', 'cols'))]
    pallas_call x0 -> x1, Pallas kernels: none -> 115 us  [local(): pl.pallas_call(kernel, out_shape=(jax.ShapeDtypeStruct((INST, COLS), F32)...]
    dot_general x6 -> x0, matrix products: 39.3 us -> none  [the longest x3 21 us: matrix_times(): lax.dot_general(primal_bf, matrix, (((1,), (1,)), ((), ())), preferred_el...]
    unnamed x22 -> x15, local copies, waits for them, and re-layouts: 0.05 us -> 11.2 us
  transfers between devices with their start and end apart: 5 -> 0, of which waited for: 5 -> 0; matrix products, arithmetic and copies ran while one was open for 0% -> 0% of each run, Pallas kernels for 0% -> 0%
where the time goes in v1:
time: 129 us; the launch traced here: 126 us
  Pallas kernels  115 us (89%)
  local copies, waits for them, and re-layouts  11.2 us (9%)
    pallas_call x1, Pallas kernels, local(): pl.pallas_call(kernel, out_shape=(jax.ShapeDtypeStruct((INST, COLS), F32)...  115 us
    unnamed x15, local copies, waits for them, and re-layouts  11.2 us

profile of v1, /device:TPU:1, one launch (start us, length us, event | category | flops | bytes accessed | tf_op | source)
XLA Modules:
  0.0 126.5 jit_solution(12137219848155171667)
XLA Ops:
  0.6 0.8 copy.11.numer_ref
  1.4 0.8 copy.12.denom_ref
  2.2 0.0 copy-start
  2.2 1.0 copy-done
  3.2 0.0 copy-start.1
  3.2 1.0 copy-done.1
  4.3 0.0 copy-start.2
  4.3 0.9 copy-done.2
  5.2 0.0 copy-start.3
  5.2 0.7 copy-done.3
  5.9 0.0 copy-start.4
  5.9 0.7 copy-done.4
  6.6 114.6 %shard_map.103 = (f32[64,4096]{1,0:T(8,128)}, f32[64,1024]{1,0:T(8,128)S(1)}, f32[64,4096]{1,0:T(8,128)}) custom-call(bf16[1024,4096]{1,0:T(8,128)(2,1)} %m_hbm.1, bf16[64,4096]{1,0:T(8,128)(2,1)S(1)} %copy-done, bf16[64,4096]{1,0:T(8,128)(2,1)S(1)} %copy-done.1, f32[64,1024]{1,0:T(8,128)S(1)} %copy-done.2, f32[1,1024]{1,0:T(1,128)S(1)} %bitcast.3, ...), custom_call_target="tpu_custom_call" | custom-call | tf_op jit(solution)/shard_map/pallas_call | solution.py:403
  121.3 2.3 %copy.16 = f32[64,4096]{1,0:T(8,128)} copy(f32[64,4096]{1,0:T(8,128)} %get-tuple-element.6) | data formatting | bytes 2097152
  123.5 0.7 copy.17
  124.2 2.3 %copy.18 = f32[64,4096]{1,0:T(8,128)} copy(f32[64,4096]{1,0:T(8,128)} %get-tuple-element.8) | data formatting | bytes 2097152
Async XLA Ops:
  2.2 1.0 copy-start
  3.2 1.0 copy-start.1
  4.3 0.9 copy-start.2
  5.2 0.7 copy-start.3
  5.9 0.7 copy-start.4

commit v2 on v1

v2 whole, which is shorter than its diff:
```python
import jax
import jax.numpy as jnp
from jax import lax
from jax.experimental import pallas as pl
from jax.experimental.pallas import tpu as pltpu
from jax.sharding import PartitionSpec as P

VARS = 65536
MESH = pl.DeviceIdType.MESH
F32 = jnp.float32
BF16 = jnp.bfloat16
SHARP = 16.0
EPS = 1e-06

INST = 64
HALF = 32
ROWS = 1024
COLS = 4096
SIDE = 4
WIDE = COLS // SIDE
CHUNK = WIDE // SIDE
TEAM = 8
PIECE = ROWS // TEAM
LANES = 128


def kernel(
    m_hbm, cp_hbm, ct_hbm, d0_hbm, right_hbm, code_hbm, numer_hbm, denom_hbm,
    primal_out, dual_out, grad_out,
    primal_ref, dual_ref, grad_ref, out_sem, m_ref, m_sem, cp_ref, ct_ref, d0_ref, right_ref, code_ref, numer_ref, denom_ref, in_sem,
    tau_ref, sigma_ref, theta_ref, scale2_ref, low_ref, high_ref, sum_ref,
    dbf_ref, own0_ref, own1_ref, t0_ref, t1_ref, red0_ref, sh0_ref, slope0_ref, sa1_ref, e_ref, z_ref,
    s1x, s1z, r1x, r1z, s2z, s2x, r2z, r2x, gather,
    a_ss, a_rs, s_ss, s_rs, f_ss, f_rs,
    sb, rb, zs, zr, gb, gd,
    b_ss, b_rs, z_ss, z_rs, g_ss, g_rs, gd_ss, gd_rs,
    rows_t, rows_p, rows_pr, rowx, rowz,
    t_ss, t_rs, p_ss, p_rs, rx_ss, rx_rs, rz_ss, rz_rs,
    dual1_ref, weigh_ref, wimg_ref,
):
    rr = lax.axis_index("rows")
    cc = lax.axis_index("cols")
    x, zl = rr // SIDE, lax.rem(rr, SIDE)
    zh, yc = cc // TEAM, lax.rem(cc, TEAM)
    y = yc // 2

    def flip(value, k):
        if k == 0:
            return value
        total = value
        for bit in (1, 2, 4):
            if k & bit:
                total = total + bit - 2 * bit * lax.rem(value // bit, 2)
        return total

    def x_peer(k):
        return (flip(x, k) * SIDE + zl, cc)

    def z_peer(k):
        return (x * SIDE + flip(zl, k), cc)

    def team_peer(k):
        return (rr, zh * TEAM + flip(yc, k))

    far_peer = (rr, (1 - zh) * TEAM + yc)

    def remote(src, dst, send, recv, peer):
        copy = pltpu.make_async_remote_copy(
            src_ref=src, dst_ref=dst, send_sem=send, recv_sem=recv, device_id=peer, device_id_type=MESH
        )
        copy.start()
        return copy

    def at(value, size):
        return pl.ds(pl.multiple_of(value * size, size), size)

    order = (2, 1, 3, 0)
    near_last = (2, 3, 1)
    team_order = (4, 5, 6, 7, 2, 3, 1)

    def load(n, src, dst):
        copy = pltpu.make_async_copy(src, dst, in_sem.at[n])
        copy.start()
        return copy

    load_d0 = load(0, d0_hbm, d0_ref)
    load_cp = load(1, cp_hbm, cp_ref)
    m_loads = []
    for k in order:
        cols = at(flip(x, k), WIDE)
        copy = pltpu.make_async_copy(m_hbm.at[:, cols], m_ref.at[:, cols], m_sem.at[k])
        copy.start()
        m_loads.append(copy)
    small_loads = [
        load(2, right_hbm, right_ref), load(3, code_hbm, code_ref),
        load(4, numer_hbm, numer_ref), load(5, denom_hbm, denom_ref),
    ]
    load_ct = load(6, ct_hbm, ct_ref)

    barrier = pltpu.get_barrier_semaphore()
    for k in (1, 2, 3):
        pl.semaphore_signal(barrier, inc=1, device_id=x_peer(k), device_id_type=MESH)
        pl.semaphore_signal(barrier, inc=1, device_id=z_peer(k), device_id_type=MESH)
    for k in range(1, TEAM):
        pl.semaphore_signal(barrier, inc=1, device_id=team_peer(k), device_id_type=MESH)
    pl.semaphore_signal(barrier, inc=1, device_id=far_peer, device_id_type=MESH)

    lane = lax.broadcasted_iota(jnp.int32, (INST, LANES), 1)
    diagonal = lane == lax.broadcasted_iota(jnp.int32, (INST, LANES), 0)

    def to_row(column):
        spread = jnp.where(diagonal, jnp.broadcast_to(column, (INST, LANES)), 0.0)
        return jnp.broadcast_to(jnp.sum(spread, axis=0, keepdims=True), (8, LANES))

    def to_column(row):
        spread = jnp.where(diagonal, jnp.broadcast_to(row[0:1, :], (INST, LANES)), 0.0)
        return jnp.sum(spread, axis=1, keepdims=True)

    square = lax.broadcasted_iota(jnp.int32, (INST, INST), 1) == lax.broadcasted_iota(jnp.int32, (INST, INST), 0)

    def ratio(n):
        row = numer_ref[n : n + 1, :].astype(F32) / denom_ref[n : n + 1, :].astype(F32)
        return jnp.sum(jnp.where(square, jnp.broadcast_to(row, (INST, INST)), 0.0), axis=1, keepdims=True)

    def spread(column):
        return jnp.broadcast_to(column, (INST, LANES))

    def wait_all(copies):
        for c in copies:
            c.wait()

    def team_rows(which):
        return [
            remote(rows_t.at[which, yc], rows_t.at[which, yc], t_ss.at[which, k - 1], t_rs.at[which, k - 1], team_peer(k))
            for k in team_order
        ]

    def sum_team(which):
        total = rows_t[which, 0]
        for i in range(1, TEAM):
            total = total + rows_t[which, i]
        return total

    def far_row(which):
        return remote(rows_p.at[which], rows_pr.at[which], p_ss.at[which], p_rs.at[which], far_peer)

    def product(k):
        j = flip(x, k)
        out = jnp.dot(dbf_ref[...], m_ref[:, at(j, WIDE)], preferred_element_type=F32)
        if k:
            s1x[k - 1] = out[:HALF].astype(BF16)
        else:
            own0_ref[...] = out[:HALF]
        own1_ref[j] = out[HALF:]
        for q in near_last:
            s1z[q - 1, j] = own1_ref[j, :, at(flip(zl, q), CHUNK)].astype(BF16)

    def send_product(k):
        j = flip(x, k)
        sent_x = None
        if k:
            sent_x = remote(s1x.at[k - 1], r1x.at[k - 1], a_ss.at[0, k - 1], a_rs.at[0, k - 1], x_peer(k))
        sent_z = [
            remote(s1z.at[q - 1, j], r1z.at[q - 1, j], s_ss.at[q - 1, k], s_rs.at[q - 1, k], z_peer(q)) for q in near_last
        ]
        return sent_x, sent_z

    def scatter_dual():
        sends = {}
        for k in order:
            product(k)
            sends[k] = send_product(k)
        return sends

    def second_dual(sends):
        later = []

        def finish_z(k):
            j = flip(x, k)
            wait_all(sends[k][1])
            total = own1_ref[j, :, at(zl, CHUNK)]
            for q in range(3):
                total = total + r1z[q, j].astype(F32)
            if k:
                s2x[k - 1] = total.astype(BF16)
                later.append(remote(s2x.at[k - 1], r2x.at[k - 1], a_ss.at[3, k - 1], a_rs.at[3, k - 1], x_peer(k)))
            else:
                t1_ref[...] = total

        finish_z(2)
        finish_z(1)
        for k in (1, 2, 3):
            sends[k][0].wait()
        t0_ref[...] = own0_ref[...] + r1x[0].astype(F32) + r1x[1].astype(F32) + r1x[2].astype(F32)
        for k in near_last:
            s2z[k - 1] = t0_ref[:, at(flip(zl, k), CHUNK)].astype(BF16)
            later.append(remote(s2z.at[k - 1], r2z.at[k - 1], a_ss.at[2, k - 1], a_rs.at[2, k - 1], z_peer(k)))
        finish_z(3)
        finish_z(0)
        return later

    def gather_dual(later, process, aside=None):
        wait_all(later)
        upper = t0_ref[:, at(zl, CHUNK)] + r2z[0].astype(F32) + r2z[1].astype(F32) + r2z[2].astype(F32)
        lower = t1_ref[...] + r2x[0].astype(F32) + r2x[1].astype(F32) + r2x[2].astype(F32)
        gather[x, zl, :HALF] = upper.astype(BF16)
        gather[x, zl, HALF:] = lower.astype(BF16)
        mine = gather.at[x, zl]
        z_own = {}
        x_own = {}
        for k in near_last:
            z_own[k] = remote(mine, mine, a_ss.at[4, k - 1], a_rs.at[4, k - 1], z_peer(k))
            x_own[k] = remote(mine, mine, a_ss.at[5, k - 1], a_rs.at[5, k - 1], x_peer(k))
        process(x, zl)
        from_x = {}
        from_z = {}
        for k in (1, 3, 2):
            z_own[k].wait()
            part = gather.at[x, flip(zl, k), pl.ds(0, HALF)]
            for q in near_last:
                from_x[q, k] = remote(part, part, f_ss.at[0, k - 1, q - 1], f_rs.at[0, k - 1, q - 1], x_peer(q))
            x_own[k].wait()
            part = gather.at[flip(x, k), zl, pl.ds(HALF, HALF)]
            for q in near_last:
                from_z[k, q] = remote(part, part, f_ss.at[1, k - 1, q - 1], f_rs.at[1, k - 1, q - 1], z_peer(q))
            if k != 2:
                process(x, flip(zl, k))
                process(flip(x, k), zl)
        process(x, flip(zl, 2))
        process(flip(x, 2), zl)
        if aside is not None:
            aside()
        for qx, qz in ((1, 1), (3, 1), (1, 3), (3, 3), (2, 1), (1, 2), (2, 3), (3, 2), (2, 2)):
            from_x[qx, qz].wait()
            from_z[qx, qz].wait()
            process(flip(x, qx), flip(zl, qz))

    def halves(body):
        def process(gx, gz):
            for part in range(CHUNK // LANES):
                cols = at((gx * SIDE + gz) * (CHUNK // LANES) + part, LANES)
                image = gather[gx, gz, :, part * LANES : (part + 1) * LANES].astype(F32)
                body(image, cols)

        return process

    def with_product(body, rows, uses):
        done = halves(body)
        started = []

        def process(gx, gz):
            done(gx, gz)
            cols = at(gx * SIDE + gz, CHUNK)
            out = lax.dot_general(
                e_ref[rows, cols], m_ref[:, cols], (((1,), (1,)), ((), ())), preferred_element_type=F32
            )
            for n, u in enumerate(uses):
                for i in range(TEAM):
                    part = out[n * INST : (n + 1) * INST, i * PIECE : (i + 1) * PIECE]
                    if started:
                        z_ref[u, i] += part
                    else:
                        z_ref[u, i] = part
            started.append(True)

        return process

    def scatter_primal(u):
        sends = []
        for k in team_order:
            sb[u, k - 1] = z_ref[u, flip(yc, k)].astype(BF16)
            sends.append(remote(sb.at[u, k - 1], rb.at[u, k - 1], b_ss.at[u, k - 1], b_rs.at[u, k - 1], team_peer(k)))
        return sends

    def far_primal(u, sends):
        wait_all(sends)
        total = z_ref[u, yc]
        for k in range(1, TEAM):
            total = total + rb[u, k - 1].astype(F32)
        zs[u] = total.astype(BF16)
        return remote(zs.at[u], zr.at[u], z_ss.at[u], z_rs.at[u], far_peer)

    def done_primal(u, copy):
        copy.wait()
        return zs[u].astype(F32) + zr[u].astype(F32)

    def gather_primal(v):
        return [
            remote(gb.at[v, yc], gb.at[v, yc], g_ss.at[v, k - 1], g_rs.at[v, k - 1], team_peer(k)) for k in team_order
        ]

    def fill_dual(v):
        for i in range(TEAM):
            dbf_ref[:, i * PIECE : (i + 1) * PIECE] = gb[v, i]

    own_cols = at(yc, PIECE)

    load_d0.wait()
    dbf_ref[...] = d0_ref[...].astype(BF16)
    load_cp.wait()
    sum_ref[...] = jnp.zeros_like(sum_ref)

    def square_step(i, _):
        c = cp_ref[:, at(i, LANES)].astype(F32)
        sum_ref[...] += c * c
        return 0

    lax.fori_loop(0, COLS // LANES, square_step, 0, unroll=4)
    rows_t[0, yc] = to_row(jnp.sum(sum_ref[...], axis=1, keepdims=True))
    for position, k in enumerate(order):
        m_loads[position].wait()
        product(k)
    pl.semaphore_wait(barrier, 14)
    sends = {k: send_product(k) for k in order}
    norm_copies = team_rows(0)

    wait_all(small_loads)
    load_ct.wait()
    code = code_ref[...]
    half_code = code // 2
    low_ref[...] = -0.25 - 0.75 * (code - 2 * half_code).astype(F32)
    high_ref[...] = 0.25 + 0.75 * half_code.astype(F32)
    theta_ref[...] = spread(ratio(2))
    wait_all(norm_copies)
    rows_p[0] = sum_team(0)
    norm_far = far_row(0)
    later = second_dual(sends)
    norm_far.wait()
    norm_sum = to_column(rows_p[0] + rows_pr[0])
    scale = jnp.sqrt(norm_sum / VARS + EPS)
    tau_ref[...] = spread(ratio(0) / scale)
    sigma_ref[...] = spread(ratio(1) * scale)
    scale2_ref[...] = spread(VARS * scale * scale)

    def first_step(image, cols):
        reduced = cp_ref[:, cols].astype(F32) - image
        shifted = 0.0 - tau_ref[...] * reduced
        projected = jnp.minimum(jnp.maximum(shifted, low_ref[:, cols]), high_ref[:, cols])
        red0_ref[:, cols] = reduced
        sh0_ref[:, cols] = shifted
        e_ref[:INST, cols] = (projected + theta_ref[...] * projected).astype(BF16)

    gather_dual(later, with_product(first_step, slice(0, INST), (0,)))

    sends = scatter_primal(0)

    def slope_of(shifted, cols):
        return jax.nn.sigmoid(SHARP * (shifted - low_ref[:, cols])) * jax.nn.sigmoid(
            SHARP * (high_ref[:, cols] - shifted)
        )

    def slope_step(i, _):
        cols = at(i, LANES)
        slope = slope_of(sh0_ref[:, cols], cols)
        slope0_ref[:, cols] = slope
        e_ref[INST:, cols] = (slope * red0_ref[:, cols]).astype(BF16)
        return 0

    lax.fori_loop(0, COLS // LANES, slope_step, 0, unroll=2)
    far = far_primal(0, sends)
    for i in range(SIDE):
        out = lax.dot_general(
            e_ref[INST:, :], m_ref[i * 2 * PIECE : (i + 1) * 2 * PIECE, :], (((1,), (1,)), ((), ())),
            preferred_element_type=F32,
        )
        z_ref[1, 2 * i] = out[:, :PIECE]
        z_ref[1, 2 * i + 1] = out[:, PIECE:]
    image = done_primal(0, far)
    residue0 = right_ref[:, own_cols] - image
    dual1 = d0_ref[:, own_cols] + sigma_ref[...] * residue0
    gb[0, yc] = dual1.astype(BF16)
    gathers = gather_primal(0)
    weigh_sends = scatter_primal(1)
    dual1_ref[...] = dual1
    weigh_ref[...] = sigma_ref[...] * residue0
    wait_all(gathers)
    fill_dual(0)

    sends = scatter_dual()
    weigh_far = far_primal(1, weigh_sends)
    later = second_dual(sends)
    wimg_ref[...] = tau_ref[...] * (1.0 + theta_ref[...]) * sigma_ref[...] * done_primal(1, weigh_far)
    sum_ref[...] = jnp.zeros_like(sum_ref)

    def second_step(image, cols):
        low, high = low_ref[:, cols], high_ref[:, cols]
        reduced = cp_ref[:, cols].astype(F32) - image
        before = jnp.minimum(jnp.maximum(sh0_ref[:, cols], low), high)
        shifted = before - tau_ref[...] * reduced
        projected = jnp.minimum(jnp.maximum(shifted, low), high)
        primal_ref[:, cols] = projected
        e_ref[INST:, cols] = (projected + theta_ref[...] * (projected - before)).astype(BF16)
        slope_adj = slope_of(shifted, cols) * ct_ref[:, cols].astype(F32)
        sa1_ref[:, cols] = slope_adj
        e_ref[:INST, cols] = (tau_ref[...] * slope_adj).astype(BF16)
        sum_ref[...] += slope_adj * reduced + slope_adj * (slope0_ref[:, cols] * red0_ref[:, cols])

    gather_dual(later, with_product(second_step, slice(0, 2 * INST), (2, 3)))

    primal_copy = pltpu.make_async_copy(primal_ref, primal_out, out_sem.at[0])

    sends = scatter_primal(2)
    rows_t[1, yc] = to_row(tau_ref[:, 0:1] * jnp.sum(sum_ref[...], axis=1, keepdims=True))
    factor_copies = team_rows(1)
    primal_copy.start()
    far = far_primal(2, sends)
    end_sends = scatter_primal(3)
    wait_all(factor_copies)
    rows_p[1] = sum_team(1)
    factor_far = far_row(1)
    adjoint = done_primal(2, far)
    rounded = adjoint.astype(BF16)
    gb[1, yc] = rounded
    gathers = gather_primal(1)
    weighed = adjoint * weigh_ref[...] - rounded.astype(F32) * wimg_ref[...]
    rows_t[2, yc] = to_row(jnp.sum(weighed, axis=1, keepdims=True))
    factor_copies = team_rows(2)
    wait_all(gathers)
    fill_dual(1)

    sends = scatter_dual()
    end_far = far_primal(3, end_sends)
    wait_all(factor_copies)
    rowx[x] = sum_team(2)
    x_rows = [remote(rowx.at[x], rowx.at[x], rx_ss.at[k - 1], rx_rs.at[k - 1], x_peer(k)) for k in (1, 2, 3)]
    later = second_dual(sends)
    wait_all(x_rows)
    rowz[zl] = rowx[0] + rowx[1] + rowx[2] + rowx[3]
    z_rows = [remote(rowz.at[zl], rowz.at[zl], rz_ss.at[k - 1], rz_rs.at[k - 1], z_peer(k)) for k in (1, 2, 3)]
    factor_far.wait()
    residue1 = right_ref[:, own_cols] - done_primal(3, end_far)
    gd[yc] = dual1_ref[...] + sigma_ref[...] * residue1
    dual_gathers = [
        remote(gd.at[yc], gd.at[yc], gd_ss.at[k - 1], gd_rs.at[k - 1], team_peer(k)) for k in team_order
    ]
    wait_all(z_rows)
    factors = to_column(rows_p[1] + rows_pr[1] + (rowz[0] + rowz[1] + rowz[2] + rowz[3]))
    sum_ref[...] = spread(factors) / scale2_ref[...]

    def last_step(image, cols):
        slope_adj = sa1_ref[:, cols]
        ahead = slope_adj - (1.0 + theta_ref[...]) * (sigma_ref[...] * image)
        gradient = tau_ref[...] * (slope_adj + slope0_ref[:, cols] * ahead)
        grad_ref[:, cols] = cp_ref[:, cols].astype(F32) * sum_ref[...] - gradient

    grad_process = halves(last_step)
    out_copies = []

    def process(gx, gz):
        grad_process(gx, gz)
        cols = at(gx * SIDE + gz, CHUNK)
        copy = pltpu.make_async_copy(grad_ref.at[:, cols], grad_out.at[:, cols], out_sem.at[2 + len(out_copies)])
        copy.start()
        out_copies.append(copy)

    dual_copy = pltpu.make_async_copy(dual_ref, dual_out, out_sem.at[1])

    def dual_end():
        wait_all(dual_gathers)
        for i in range(TEAM):
            dual_ref[:, i * PIECE : (i + 1) * PIECE] = gd[i]
        dual_copy.start()

    gather_dual(later, process, dual_end)
    primal_copy.wait()
    dual_copy.wait()
    wait_all(out_copies)


def keep(a, b, c, out_a, out_b, out_c, sem):
    copies = [pltpu.make_async_copy(b, out_b, sem.at[8])]
    for n in range(4):
        rows = pl.ds(n * 16, 16)
        copies.append(pltpu.make_async_copy(a.at[rows], out_a.at[rows], sem.at[n]))
        copies.append(pltpu.make_async_copy(c.at[rows], out_c.at[rows], sem.at[4 + n]))
    for copy in copies:
        copy.start()
    for copy in copies:
        copy.wait()


def local(matrix, cost_pred, cost_true, dual_start, right_side, bound_code, step_numer, step_denom):
    dma = pltpu.SemaphoreType.DMA
    v = pltpu.VMEM
    anywhere = pl.BlockSpec(memory_space=pl.ANY)
    uses, rows = 4, 3
    scratch = [
        v((INST, COLS), F32), v((INST, ROWS), F32), v((INST, COLS), F32), dma((2 + SIDE * SIDE,)),
        v((ROWS, COLS), BF16), dma((SIDE,)), v((INST, COLS), BF16), v((INST, COLS), BF16), v((INST, ROWS), F32),
        v((1, ROWS), F32), v((1, COLS), jnp.int32), v((3, INST), jnp.int32), v((3, INST), jnp.int32), dma((7,)),
        v((INST, LANES), F32), v((INST, LANES), F32), v((INST, LANES), F32), v((INST, LANES), F32),
        v((1, COLS), F32), v((1, COLS), F32), v((INST, LANES), F32),
        v((INST, ROWS), BF16), v((HALF, WIDE), F32), v((SIDE, HALF, WIDE), F32), v((HALF, WIDE), F32),
        v((HALF, CHUNK), F32), v((INST, COLS), F32), v((INST, COLS), F32), v((INST, COLS), F32),
        v((INST, COLS), F32), v((2 * INST, COLS), BF16), v((uses, TEAM, INST, PIECE), F32),
        v((3, HALF, WIDE), BF16), v((3, SIDE, HALF, CHUNK), BF16), v((3, HALF, WIDE), BF16), v((3, SIDE, HALF, CHUNK), BF16),
        v((3, HALF, CHUNK), BF16), v((3, HALF, CHUNK), BF16), v((3, HALF, CHUNK), BF16), v((3, HALF, CHUNK), BF16),
        v((SIDE, SIDE, INST, CHUNK), BF16),
        dma((6, 3)), dma((6, 3)), dma((3, SIDE)), dma((3, SIDE)), dma((2, 3, 3)), dma((2, 3, 3)),
        v((uses, TEAM - 1, INST, PIECE), BF16), v((uses, TEAM - 1, INST, PIECE), BF16),
        v((uses, INST, PIECE), BF16), v((uses, INST, PIECE), BF16),
        v((2, TEAM, INST, PIECE), BF16), v((TEAM, INST, PIECE), F32),
        dma((uses, TEAM - 1)), dma((uses, TEAM - 1)), dma((uses,)), dma((uses,)),
        dma((2, TEAM - 1)), dma((2, TEAM - 1)), dma((TEAM - 1,)), dma((TEAM - 1,)),
        v((rows, TEAM, 8, LANES), F32), v((2, 8, LANES), F32), v((2, 8, LANES), F32), v((SIDE, 8, LANES), F32),
        v((SIDE, 8, LANES), F32),
        dma((rows, TEAM - 1)), dma((rows, TEAM - 1)), dma((2,)), dma((2,)), dma((3,)), dma((3,)), dma((3,)), dma((3,)),
        v((INST, PIECE), F32), v((INST, PIECE), F32), v((INST, PIECE), F32),
    ]
    outs = (
        jax.ShapeDtypeStruct((INST, COLS), F32),
        jax.ShapeDtypeStruct((INST, ROWS), F32),
        jax.ShapeDtypeStruct((INST, COLS), F32),
    )
    results = pl.pallas_call(
        kernel,
        out_shape=outs,
        in_specs=[anywhere] * 8,
        out_specs=(anywhere,) * 3,
        scratch_shapes=scratch,
        compiler_params=pltpu.CompilerParams(
            collective_id=0, has_side_effects=True, vmem_limit_bytes=63 * 2**20
        ),
    )(
        matrix,
        cost_pred,
        cost_true,
        dual_start,
        right_side.reshape(1, ROWS),
        bound_code.reshape(1, COLS),
        step_numer.T,
        step_denom.T,
    )
    return pl.pallas_call(
        keep,
        out_shape=outs,
        in_specs=[anywhere] * 3,
        out_specs=(anywhere,) * 3,
        scratch_shapes=[dma((9,))],
        compiler_params=pltpu.CompilerParams(vmem_limit_bytes=63 * 2**20),
    )(*results)


def solution(mesh):
    placed = (
        P("rows", "cols"),
        P(None, "cols"),
        P(None, "cols"),
        P(None, "rows"),
        P("rows"),
        P("cols"),
        P(),
        P(),
    )
    return jax.shard_map(
        local,
        mesh=mesh,
        in_specs=placed,
        out_specs=(P(None, "cols"), P(None, "rows"), P(None, "cols")),
        check_vma=False,
    )
```

time: 129 us -> 176 us (1.36)
  Pallas kernels: 115 us -> 173 us
  local copies, waits for them, and re-layouts: 11.2 us -> 0 us
    pallas_call x1 -> x2, Pallas kernels: 115 us -> 173 us  [the longest x1 100 us: local(): pl.pallas_call(kernel, out_shape=outs, in_specs=[anywhere] * 8, out_specs...]
    unnamed x15 -> x0, local copies, waits for them, and re-layouts: 11.2 us -> none
where the time goes in v2:
time: 176 us; the launch traced here: 174 us
  Pallas kernels  173 us (98%)
    pallas_call x1, Pallas kernels, local(): pl.pallas_call(kernel, out_shape=outs, in_specs=[anywhere] * 8, out_specs...  100 us
    pallas_call x1, Pallas kernels, local(): pl.pallas_call(keep, out_shape=outs, in_specs=[anywhere] * 3, out_specs=(...  72.7 us

profile of v2, /device:TPU:1, one launch (start us, length us, event | category | flops | bytes accessed | tf_op | source)
XLA Modules:
  0.0 173.6 jit_solution(13276390074838713355)
XLA Ops:
  0.6 100.1 %shard_map.103 = (f32[64,4096]{1,0:T(8,128)}, f32[64,1024]{1,0:T(8,128)}, f32[64,4096]{1,0:T(8,128)}) custom-call(bf16[1024,4096]{1,0:T(8,128)(2,1)} %m_hbm.1, bf16[64,4096]{1,0:T(8,128)(2,1)} %cp_hbm.1, bf16[64,4096]{1,0:T(8,128)(2,1)} %ct_hbm.1, f32[64,1024]{1,0:T(8,128)} %d0_hbm.1, f32[1,1024]{1,0:T(1,128)} %bitcast.5, s32[1,4096]{1,0:T(1,128)} %bitcast.4, ...), custom_call_target="tpu_custom_call" | custom-call | tf_op jit(solution)/shard_map/pallas_call | solution.py:515
  100.7 72.7 %shard_map.104 = (f32[64,4096]{1,0:T(8,128)}, f32[64,1024]{1,0:T(8,128)}, f32[64,4096]{1,0:T(8,128)}) custom-call(f32[64,4096]{1,0:T(8,128)} %get-tuple-element.6.a, f32[64,1024]{1,0:T(8,128)} %get-tuple-element.7.b, f32[64,4096]{1,0:T(8,128)} %get-tuple-element.8.c), custom_call_target="tpu_custom_call" | custom-call | tf_op jit(solution)/shard_map/pallas_call | solution.py:534

commit v3 on v2

--- a/solution.py
+++ b/solution.py
@@ -13,7 +13,7 @@
 EPS = 1e-06
 
 INST = 64
-HALF = 32
+CUT = 80
 ROWS = 1024
 COLS = 4096
 SIDE = 4
@@ -22,6 +22,8 @@
 TEAM = 8
 PIECE = ROWS // TEAM
 LANES = 128
+STACK = INST * CHUNK // LANES
+REST = STACK - CUT
 
 
 def kernel(
@@ -29,7 +31,7 @@
     primal_out, dual_out, grad_out,
     primal_ref, dual_ref, grad_ref, out_sem, m_ref, m_sem, cp_ref, ct_ref, d0_ref, right_ref, code_ref, numer_ref, denom_ref, in_sem,
     tau_ref, sigma_ref, theta_ref, scale2_ref, low_ref, high_ref, sum_ref,
-    dbf_ref, own0_ref, own1_ref, t0_ref, t1_ref, red0_ref, sh0_ref, slope0_ref, sa1_ref, e_ref, z_ref,
+    dbf_ref, own_ref, t0_ref, t1_ref, red0_ref, sh0_ref, slope0_ref, sa1_ref, e_ref, z_ref,
     s1x, s1z, r1x, r1z, s2z, s2x, r2z, r2x, gather,
     a_ss, a_rs, s_ss, s_rs, f_ss, f_rs,
     sb, rb, zs, zr, gb, gd,
@@ -147,13 +149,14 @@
     def product(k):
         j = flip(x, k)
         out = jnp.dot(dbf_ref[...], m_ref[:, at(j, WIDE)], preferred_element_type=F32)
+        for gz in range(SIDE):
+            for part in range(CHUNK // LANES):
+                start = gz * CHUNK + part * LANES
+                own_ref[j, gz, part * INST : (part + 1) * INST] = out[:, start : start + LANES]
         if k:
-            s1x[k - 1] = out[:HALF].astype(BF16)
-        else:
-            own0_ref[...] = out[:HALF]
-        own1_ref[j] = out[HALF:]
+            s1x[k - 1] = own_ref[j, :, :CUT].astype(BF16)
         for q in near_last:
-            s1z[q - 1, j] = own1_ref[j, :, at(flip(zl, q), CHUNK)].astype(BF16)
+            s1z[q - 1, j] = own_ref[j, flip(zl, q), CUT:].astype(BF16)
 
     def send_product(k):
         j = flip(x, k)
@@ -178,7 +181,7 @@
         def finish_z(k):
             j = flip(x, k)
             wait_all(sends[k][1])
-            total = own1_ref[j, :, at(zl, CHUNK)]
+            total = own_ref[j, zl, CUT:]
             for q in range(3):
                 total = total + r1z[q, j].astype(F32)
             if k:
@@ -191,9 +194,9 @@
         finish_z(1)
         for k in (1, 2, 3):
             sends[k][0].wait()
-        t0_ref[...] = own0_ref[...] + r1x[0].astype(F32) + r1x[1].astype(F32) + r1x[2].astype(F32)
+        t0_ref[...] = own_ref[x, :, :CUT] + r1x[0].astype(F32) + r1x[1].astype(F32) + r1x[2].astype(F32)
         for k in near_last:
-            s2z[k - 1] = t0_ref[:, at(flip(zl, k), CHUNK)].astype(BF16)
+            s2z[k - 1] = t0_ref[flip(zl, k)].astype(BF16)
             later.append(remote(s2z.at[k - 1], r2z.at[k - 1], a_ss.at[2, k - 1], a_rs.at[2, k - 1], z_peer(k)))
         finish_z(3)
         finish_z(0)
@@ -201,33 +204,41 @@
 
     def gather_dual(later, process, aside=None):
         wait_all(later)
-        upper = t0_ref[:, at(zl, CHUNK)] + r2z[0].astype(F32) + r2z[1].astype(F32) + r2z[2].astype(F32)
+        upper = t0_ref[zl] + r2z[0].astype(F32) + r2z[1].astype(F32) + r2z[2].astype(F32)
         lower = t1_ref[...] + r2x[0].astype(F32) + r2x[1].astype(F32) + r2x[2].astype(F32)
-        gather[x, zl, :HALF] = upper.astype(BF16)
-        gather[x, zl, HALF:] = lower.astype(BF16)
-        mine = gather.at[x, zl]
+        gather[x, zl, :CUT] = upper.astype(BF16)
+        gather[x, zl, CUT:] = lower.astype(BF16)
+        above = pl.ds(0, CUT)
+        below = pl.ds(CUT, REST)
+        mine_above = gather.at[x, zl, above]
+        mine_below = gather.at[x, zl, below]
         z_own = {}
         x_own = {}
+        z_more = {}
+        x_more = {}
         for k in near_last:
-            z_own[k] = remote(mine, mine, a_ss.at[4, k - 1], a_rs.at[4, k - 1], z_peer(k))
-            x_own[k] = remote(mine, mine, a_ss.at[5, k - 1], a_rs.at[5, k - 1], x_peer(k))
+            z_own[k] = remote(mine_above, mine_above, a_ss.at[4, k - 1], a_rs.at[4, k - 1], z_peer(k))
+            x_own[k] = remote(mine_below, mine_below, a_ss.at[5, k - 1], a_rs.at[5, k - 1], x_peer(k))
+        for k in near_last:
+            z_more[k] = remote(mine_below, mine_below, a_ss.at[6, k - 1], a_rs.at[6, k - 1], z_peer(k))
+            x_more[k] = remote(mine_above, mine_above, a_ss.at[7, k - 1], a_rs.at[7, k - 1], x_peer(k))
         process(x, zl)
         from_x = {}
         from_z = {}
         for k in (1, 3, 2):
+            x_own[k].wait()
+            part = gather.at[flip(x, k), zl, below]
+            for q in near_last:
+                from_z[k, q] = remote(part, part, f_ss.at[1, k - 1, q - 1], f_rs.at[1, k - 1, q - 1], z_peer(q))
             z_own[k].wait()
-            part = gather.at[x, flip(zl, k), pl.ds(0, HALF)]
+            part = gather.at[x, flip(zl, k), above]
             for q in near_last:
                 from_x[q, k] = remote(part, part, f_ss.at[0, k - 1, q - 1], f_rs.at[0, k - 1, q - 1], x_peer(q))
-            x_own[k].wait()
-            part = gather.at[flip(x, k), zl, pl.ds(HALF, HALF)]
-            for q in near_last:
-                from_z[k, q] = remote(part, part, f_ss.at[1, k - 1, q - 1], f_rs.at[1, k - 1, q - 1], z_peer(q))
-            if k != 2:
-                process(x, flip(zl, k))
-                process(flip(x, k), zl)
-        process(x, flip(zl, 2))
-        process(flip(x, 2), zl)
+        for k in (1, 3, 2):
+            z_more[k].wait()
+            process(x, flip(zl, k))
+            x_more[k].wait()
+            process(flip(x, k), zl)
         if aside is not None:
             aside()
         for qx, qz in ((1, 1), (3, 1), (1, 3), (3, 3), (2, 1), (1, 2), (2, 3), (3, 2), (2, 2)):
@@ -239,7 +250,7 @@
         def process(gx, gz):
             for part in range(CHUNK // LANES):
                 cols = at((gx * SIDE + gz) * (CHUNK // LANES) + part, LANES)
-                image = gather[gx, gz, :, part * LANES : (part + 1) * LANES].astype(F32)
+                image = gather[gx, gz, part * INST : (part + 1) * INST].astype(F32)
                 body(image, cols)
 
         return process
@@ -365,12 +376,12 @@
         )
         z_ref[1, 2 * i] = out[:, :PIECE]
         z_ref[1, 2 * i + 1] = out[:, PIECE:]
+    weigh_sends = scatter_primal(1)
     image = done_primal(0, far)
     residue0 = right_ref[:, own_cols] - image
     dual1 = d0_ref[:, own_cols] + sigma_ref[...] * residue0
     gb[0, yc] = dual1.astype(BF16)
     gathers = gather_primal(0)
-    weigh_sends = scatter_primal(1)
     dual1_ref[...] = dual1
     weigh_ref[...] = sigma_ref[...] * residue0
     wait_all(gathers)
@@ -467,15 +478,20 @@
     wait_all(out_copies)
 
 
-def keep(a, b, c, out_a, out_b, out_c, sem):
-    copies = [pltpu.make_async_copy(b, out_b, sem.at[8])]
+def keep(a, b, c, out_a, out_b, out_c, hold_a, hold_b, hold_c, in_sem, out_sem):
+    ways = [(b, hold_b, out_b)]
     for n in range(4):
         rows = pl.ds(n * 16, 16)
-        copies.append(pltpu.make_async_copy(a.at[rows], out_a.at[rows], sem.at[n]))
-        copies.append(pltpu.make_async_copy(c.at[rows], out_c.at[rows], sem.at[4 + n]))
-    for copy in copies:
+        ways.append((a.at[rows], hold_a.at[rows], out_a.at[rows]))
+        ways.append((c.at[rows], hold_c.at[rows], out_c.at[rows]))
+    loads = [pltpu.make_async_copy(src, hold, in_sem.at[n]) for n, (src, hold, _) in enumerate(ways)]
+    stores = [pltpu.make_async_copy(hold, dst, out_sem.at[n]) for n, (_, hold, dst) in enumerate(ways)]
+    for copy in loads:
         copy.start()
-    for copy in copies:
+    for load, store in zip(loads, stores):
+        load.wait()
+        store.start()
+    for copy in stores:
         copy.wait()
 
 
@@ -490,13 +506,13 @@
         v((1, ROWS), F32), v((1, COLS), jnp.int32), v((3, INST), jnp.int32), v((3, INST), jnp.int32), dma((7,)),
         v((INST, LANES), F32), v((INST, LANES), F32), v((INST, LANES), F32), v((INST, LANES), F32),
         v((1, COLS), F32), v((1, COLS), F32), v((INST, LANES), F32),
-        v((INST, ROWS), BF16), v((HALF, WIDE), F32), v((SIDE, HALF, WIDE), F32), v((HALF, WIDE), F32),
-        v((HALF, CHUNK), F32), v((INST, COLS), F32), v((INST, COLS), F32), v((INST, COLS), F32),
+        v((INST, ROWS), BF16), v((SIDE, SIDE, STACK, LANES), F32), v((SIDE, CUT, LANES), F32), v((REST, LANES), F32),
+        v((INST, COLS), F32), v((INST, COLS), F32), v((INST, COLS), F32),
         v((INST, COLS), F32), v((2 * INST, COLS), BF16), v((uses, TEAM, INST, PIECE), F32),
-        v((3, HALF, WIDE), BF16), v((3, SIDE, HALF, CHUNK), BF16), v((3, HALF, WIDE), BF16), v((3, SIDE, HALF, CHUNK), BF16),
-        v((3, HALF, CHUNK), BF16), v((3, HALF, CHUNK), BF16), v((3, HALF, CHUNK), BF16), v((3, HALF, CHUNK), BF16),
-        v((SIDE, SIDE, INST, CHUNK), BF16),
-        dma((6, 3)), dma((6, 3)), dma((3, SIDE)), dma((3, SIDE)), dma((2, 3, 3)), dma((2, 3, 3)),
+        v((3, SIDE, CUT, LANES), BF16), v((3, SIDE, REST, LANES), BF16), v((3, SIDE, CUT, LANES), BF16),
+        v((3, SIDE, REST, LANES), BF16), v((3, CUT, LANES), BF16), v((3, REST, LANES), BF16), v((3, CUT, LANES), BF16),
+        v((3, REST, LANES), BF16), v((SIDE, SIDE, STACK, LANES), BF16),
+        dma((8, 3)), dma((8, 3)), dma((3, SIDE)), dma((3, SIDE)), dma((2, 3, 3)), dma((2, 3, 3)),
         v((uses, TEAM - 1, INST, PIECE), BF16), v((uses, TEAM - 1, INST, PIECE), BF16),
         v((uses, INST, PIECE), BF16), v((uses, INST, PIECE), BF16),
         v((2, TEAM, INST, PIECE), BF16), v((TEAM, INST, PIECE), F32),
@@ -536,7 +552,7 @@
         out_shape=outs,
         in_specs=[anywhere] * 3,
         out_specs=(anywhere,) * 3,
-        scratch_shapes=[dma((9,))],
+        scratch_shapes=[v((INST, COLS), F32), v((INST, ROWS), F32), v((INST, COLS), F32), dma((9,)), dma((9,))],
         compiler_params=pltpu.CompilerParams(vmem_limit_bytes=63 * 2**20),
     )(*results)
 

time: 176 us -> 99.1 us (0.56); the launches traced: 174 us -> 98.9 us
  Pallas kernels: 173 us -> 98.1 us
    pallas_call x1, Pallas kernels: 72.7 us -> 2.5 us  [local(): pl.pallas_call(keep, out_shape=outs, in_specs=[anywhere] * 3, out_specs=(...]
    pallas_call x1, Pallas kernels: 100 us -> 95.6 us  [local(): pl.pallas_call(kernel, out_shape=outs, in_specs=[anywhere] * 8, out_specs...]
where the time goes in v3:
time: 99.1 us; the launch traced here: 98.9 us
  Pallas kernels  98.1 us (99%)
    pallas_call x1, Pallas kernels, local(): pl.pallas_call(kernel, out_shape=outs, in_specs=[anywhere] * 8, out_specs...  95.6 us
    pallas_call x1, Pallas kernels, local(): pl.pallas_call(keep, out_shape=outs, in_specs=[anywhere] * 3, out_specs=(...  2.5 us

profile of v3, /device:TPU:1, one launch (start us, length us, event | category | flops | bytes accessed | tf_op | source)
XLA Modules:
  0.0 98.9 jit_solution(9593209827165488118)
XLA Ops:
  0.6 95.6 %shard_map.103 = (f32[64,4096]{1,0:T(8,128)}, f32[64,1024]{1,0:T(8,128)}, f32[64,4096]{1,0:T(8,128)}) custom-call(bf16[1024,4096]{1,0:T(8,128)(2,1)} %m_hbm.1, bf16[64,4096]{1,0:T(8,128)(2,1)} %cp_hbm.1, bf16[64,4096]{1,0:T(8,128)(2,1)} %ct_hbm.1, f32[64,1024]{1,0:T(8,128)} %d0_hbm.1, f32[1,1024]{1,0:T(1,128)} %bitcast.5, s32[1,4096]{1,0:T(1,128)} %bitcast.4, ...), custom_call_target="tpu_custom_call" | custom-call | tf_op jit(solution)/shard_map/pallas_call | solution.py:531
  96.2 2.5 %shard_map.104 = (f32[64,4096]{1,0:T(8,128)}, f32[64,1024]{1,0:T(8,128)}, f32[64,4096]{1,0:T(8,128)}) custom-call(f32[64,4096]{1,0:T(8,128)} %get-tuple-element.6.a, f32[64,1024]{1,0:T(8,128)} %get-tuple-element.7.b, f32[64,4096]{1,0:T(8,128)} %get-tuple-element.8.c), custom_call_target="tpu_custom_call" | custom-call | tf_op jit(solution)/shard_map/pallas_call | solution.py:550

commit v4 on v3

--- a/solution.py
+++ b/solution.py
@@ -22,6 +22,7 @@
 TEAM = 8
 PIECE = ROWS // TEAM
 LANES = 128
+CUT_OUT = 96
 STACK = INST * CHUNK // LANES
 REST = STACK - CUT
 
@@ -38,7 +39,7 @@
     b_ss, b_rs, z_ss, z_rs, g_ss, g_rs, gd_ss, gd_rs,
     rows_t, rows_p, rows_pr, rowx, rowz,
     t_ss, t_rs, p_ss, p_rs, rx_ss, rx_rs, rz_ss, rz_rs,
-    dual1_ref, weigh_ref, wimg_ref,
+    dual1_ref, weigh_ref, wimg_ref, far_in,
 ):
     rr = lax.axis_index("rows")
     cc = lax.axis_index("cols")
@@ -78,6 +79,7 @@
 
     order = (2, 1, 3, 0)
     near_last = (2, 3, 1)
+    far_pieces = ((1, 1), (3, 1), (1, 3), (3, 3), (2, 1), (1, 2), (2, 3), (3, 2), (2, 2))
     team_order = (4, 5, 6, 7, 2, 3, 1)
 
     def load(n, src, dst):
@@ -105,7 +107,14 @@
         pl.semaphore_signal(barrier, inc=1, device_id=z_peer(k), device_id_type=MESH)
     for k in range(1, TEAM):
         pl.semaphore_signal(barrier, inc=1, device_id=team_peer(k), device_id_type=MESH)
-    pl.semaphore_signal(barrier, inc=1, device_id=far_peer, device_id_type=MESH)
+
+    border = 1 - lax.rem((zl + 1) // 2, 2)
+    across = (x * SIDE + (SIDE - 1 - zl), (1 - zh) * TEAM + yc)
+
+    @pl.when(border == 1)
+    def _():
+        pl.semaphore_signal(barrier, inc=1, device_id=across, device_id_type=MESH)
+
 
     lane = lax.broadcasted_iota(jnp.int32, (INST, LANES), 1)
     diagonal = lane == lax.broadcasted_iota(jnp.int32, (INST, LANES), 0)
@@ -202,14 +211,14 @@
         finish_z(0)
         return later
 
-    def gather_dual(later, process, aside=None):
+    def gather_dual(later, process, aside=None, before=None, process_far=None):
         wait_all(later)
         upper = t0_ref[zl] + r2z[0].astype(F32) + r2z[1].astype(F32) + r2z[2].astype(F32)
         lower = t1_ref[...] + r2x[0].astype(F32) + r2x[1].astype(F32) + r2x[2].astype(F32)
         gather[x, zl, :CUT] = upper.astype(BF16)
         gather[x, zl, CUT:] = lower.astype(BF16)
-        above = pl.ds(0, CUT)
-        below = pl.ds(CUT, REST)
+        above = pl.ds(0, CUT_OUT)
+        below = pl.ds(CUT_OUT, STACK - CUT_OUT)
         mine_above = gather.at[x, zl, above]
         mine_below = gather.at[x, zl, below]
         z_own = {}
@@ -222,6 +231,8 @@
         for k in near_last:
             z_more[k] = remote(mine_below, mine_below, a_ss.at[6, k - 1], a_rs.at[6, k - 1], z_peer(k))
             x_more[k] = remote(mine_above, mine_above, a_ss.at[7, k - 1], a_rs.at[7, k - 1], x_peer(k))
+        if before is not None:
+            before()
         process(x, zl)
         from_x = {}
         from_z = {}
@@ -241,10 +252,10 @@
             process(flip(x, k), zl)
         if aside is not None:
             aside()
-        for qx, qz in ((1, 1), (3, 1), (1, 3), (3, 3), (2, 1), (1, 2), (2, 3), (3, 2), (2, 2)):
+        for qx, qz in far_pieces:
             from_x[qx, qz].wait()
             from_z[qx, qz].wait()
-            process(flip(x, qx), flip(zl, qz))
+            (process_far or process)(flip(x, qx), flip(zl, qz))
 
     def halves(body):
         def process(gx, gz):
@@ -255,9 +266,10 @@
 
         return process
 
+    started = set()
+
     def with_product(body, rows, uses):
         done = halves(body)
-        started = []
 
         def process(gx, gz):
             done(gx, gz)
@@ -268,13 +280,22 @@
             for n, u in enumerate(uses):
                 for i in range(TEAM):
                     part = out[n * INST : (n + 1) * INST, i * PIECE : (i + 1) * PIECE]
-                    if started:
+                    if u in started:
                         z_ref[u, i] += part
                     else:
                         z_ref[u, i] = part
-            started.append(True)
+            started.update(uses)
 
         return process
+
+    def wide_image(u):
+        for i in range(SIDE):
+            out = lax.dot_general(
+                e_ref[INST:, :], m_ref[i * 2 * PIECE : (i + 1) * 2 * PIECE, :], (((1,), (1,)), ((), ())),
+                preferred_element_type=F32,
+            )
+            z_ref[u, 2 * i] = out[:, :PIECE]
+            z_ref[u, 2 * i + 1] = out[:, PIECE:]
 
     def scatter_primal(u):
         sends = []
@@ -321,7 +342,12 @@
     for position, k in enumerate(order):
         m_loads[position].wait()
         product(k)
-    pl.semaphore_wait(barrier, 14)
+    pl.semaphore_wait(barrier, 13 + border)
+
+    @pl.when(border == 1)
+    def _():
+        pl.semaphore_signal(far_in, inc=1, device_id=across, device_id_type=MESH)
+
     sends = {k: send_product(k) for k in order}
     norm_copies = team_rows(0)
 
@@ -332,16 +358,29 @@
     low_ref[...] = -0.25 - 0.75 * (code - 2 * half_code).astype(F32)
     high_ref[...] = 0.25 + 0.75 * half_code.astype(F32)
     theta_ref[...] = spread(ratio(2))
+
+    @pl.when(border == 1)
+    def _():
+        pl.semaphore_wait(far_in, 1)
+        pl.semaphore_signal(far_in, inc=1, device_id=z_peer(1), device_id_type=MESH)
+
     wait_all(norm_copies)
     rows_p[0] = sum_team(0)
+    later = second_dual(sends)
+
+    @pl.when(border == 0)
+    def _():
+        pl.semaphore_wait(far_in, 1)
+
     norm_far = far_row(0)
-    later = second_dual(sends)
-    norm_far.wait()
-    norm_sum = to_column(rows_p[0] + rows_pr[0])
-    scale = jnp.sqrt(norm_sum / VARS + EPS)
-    tau_ref[...] = spread(ratio(0) / scale)
-    sigma_ref[...] = spread(ratio(1) * scale)
-    scale2_ref[...] = spread(VARS * scale * scale)
+
+    def steps_of_scale():
+        norm_far.wait()
+        norm_sum = to_column(rows_p[0] + rows_pr[0])
+        scale = jnp.sqrt(norm_sum / VARS + EPS)
+        tau_ref[...] = spread(ratio(0) / scale)
+        sigma_ref[...] = spread(ratio(1) * scale)
+        scale2_ref[...] = spread(VARS * scale * scale)
 
     def first_step(image, cols):
         reduced = cp_ref[:, cols].astype(F32) - image
@@ -351,7 +390,7 @@
         sh0_ref[:, cols] = shifted
         e_ref[:INST, cols] = (projected + theta_ref[...] * projected).astype(BF16)
 
-    gather_dual(later, with_product(first_step, slice(0, INST), (0,)))
+    gather_dual(later, with_product(first_step, slice(0, INST), (0,)), before=steps_of_scale)
 
     sends = scatter_primal(0)
 
@@ -360,23 +399,7 @@
             SHARP * (high_ref[:, cols] - shifted)
         )
 
-    def slope_step(i, _):
-        cols = at(i, LANES)
-        slope = slope_of(sh0_ref[:, cols], cols)
-        slope0_ref[:, cols] = slope
-        e_ref[INST:, cols] = (slope * red0_ref[:, cols]).astype(BF16)
-        return 0
-
-    lax.fori_loop(0, COLS // LANES, slope_step, 0, unroll=2)
     far = far_primal(0, sends)
-    for i in range(SIDE):
-        out = lax.dot_general(
-            e_ref[INST:, :], m_ref[i * 2 * PIECE : (i + 1) * 2 * PIECE, :], (((1,), (1,)), ((), ())),
-            preferred_element_type=F32,
-        )
-        z_ref[1, 2 * i] = out[:, :PIECE]
-        z_ref[1, 2 * i + 1] = out[:, PIECE:]
-    weigh_sends = scatter_primal(1)
     image = done_primal(0, far)
     residue0 = right_ref[:, own_cols] - image
     dual1 = d0_ref[:, own_cols] + sigma_ref[...] * residue0
@@ -388,44 +411,71 @@
     fill_dual(0)
 
     sends = scatter_dual()
-    weigh_far = far_primal(1, weigh_sends)
+    def slope_step(i, _):
+        cols = at(i, LANES)
+        slope = slope_of(sh0_ref[:, cols], cols)
+        slope0_ref[:, cols] = slope
+        e_ref[INST:, cols] = (slope * red0_ref[:, cols]).astype(BF16)
+        return 0
+
+    lax.fori_loop(0, COLS // LANES, slope_step, 0, unroll=2)
+    wide_image(1)
+    weigh_sends = scatter_primal(1)
     later = second_dual(sends)
-    wimg_ref[...] = tau_ref[...] * (1.0 + theta_ref[...]) * sigma_ref[...] * done_primal(1, weigh_far)
-    sum_ref[...] = jnp.zeros_like(sum_ref)
 
     def second_step(image, cols):
         low, high = low_ref[:, cols], high_ref[:, cols]
         reduced = cp_ref[:, cols].astype(F32) - image
         before = jnp.minimum(jnp.maximum(sh0_ref[:, cols], low), high)
         shifted = before - tau_ref[...] * reduced
-        projected = jnp.minimum(jnp.maximum(shifted, low), high)
-        primal_ref[:, cols] = projected
-        e_ref[INST:, cols] = (projected + theta_ref[...] * (projected - before)).astype(BF16)
+        primal_ref[:, cols] = shifted
+        grad_ref[:, cols] = reduced
         slope_adj = slope_of(shifted, cols) * ct_ref[:, cols].astype(F32)
         sa1_ref[:, cols] = slope_adj
         e_ref[:INST, cols] = (tau_ref[...] * slope_adj).astype(BF16)
-        sum_ref[...] += slope_adj * reduced + slope_adj * (slope0_ref[:, cols] * red0_ref[:, cols])
-
-    gather_dual(later, with_product(second_step, slice(0, 2 * INST), (2, 3)))
-
+
+    def primal_step(image, cols):
+        low, high = low_ref[:, cols], high_ref[:, cols]
+        before = jnp.minimum(jnp.maximum(sh0_ref[:, cols], low), high)
+        projected = jnp.minimum(jnp.maximum(primal_ref[:, cols], low), high)
+        primal_ref[:, cols] = projected
+        e_ref[INST:, cols] = (projected + theta_ref[...] * (projected - before)).astype(BF16)
+        slope_adj = sa1_ref[:, cols]
+        sum_ref[...] += slope_adj * grad_ref[:, cols] + slope_adj * (slope0_ref[:, cols] * red0_ref[:, cols])
+
+    def both_steps(image, cols):
+        second_step(image, cols)
+        primal_step(image, cols)
+
+    sum_ref[...] = jnp.zeros_like(sum_ref)
+    gather_dual(
+        later,
+        with_product(both_steps, slice(0, 2 * INST), (2, 3)),
+        process_far=with_product(second_step, slice(0, INST), (2,)),
+    )
+
+    sends = scatter_primal(2)
+    weigh_far = far_primal(1, weigh_sends)
+    primal_process = with_product(primal_step, slice(INST, 2 * INST), (3,))
+    for qx, qz in far_pieces:
+        primal_process(flip(x, qx), flip(zl, qz))
     primal_copy = pltpu.make_async_copy(primal_ref, primal_out, out_sem.at[0])
-
-    sends = scatter_primal(2)
+    primal_copy.start()
     rows_t[1, yc] = to_row(tau_ref[:, 0:1] * jnp.sum(sum_ref[...], axis=1, keepdims=True))
-    factor_copies = team_rows(1)
-    primal_copy.start()
     far = far_primal(2, sends)
     end_sends = scatter_primal(3)
-    wait_all(factor_copies)
-    rows_p[1] = sum_team(1)
-    factor_far = far_row(1)
+    factor_copies = team_rows(1)
     adjoint = done_primal(2, far)
     rounded = adjoint.astype(BF16)
     gb[1, yc] = rounded
     gathers = gather_primal(1)
+    wimg_ref[...] = tau_ref[...] * (1.0 + theta_ref[...]) * sigma_ref[...] * done_primal(1, weigh_far)
     weighed = adjoint * weigh_ref[...] - rounded.astype(F32) * wimg_ref[...]
     rows_t[2, yc] = to_row(jnp.sum(weighed, axis=1, keepdims=True))
+    wait_all(factor_copies)
     factor_copies = team_rows(2)
+    rows_p[1] = sum_team(1)
+    factor_far = far_row(1)
     wait_all(gathers)
     fill_dual(1)
 
@@ -521,7 +571,7 @@
         v((rows, TEAM, 8, LANES), F32), v((2, 8, LANES), F32), v((2, 8, LANES), F32), v((SIDE, 8, LANES), F32),
         v((SIDE, 8, LANES), F32),
         dma((rows, TEAM - 1)), dma((rows, TEAM - 1)), dma((2,)), dma((2,)), dma((3,)), dma((3,)), dma((3,)), dma((3,)),
-        v((INST, PIECE), F32), v((INST, PIECE), F32), v((INST, PIECE), F32),
+        v((INST, PIECE), F32), v((INST, PIECE), F32), v((INST, PIECE), F32), pltpu.SemaphoreType.REGULAR,
     ]
     outs = (
         jax.ShapeDtypeStruct((INST, COLS), F32),

time: 99.1 us -> 97.8 us (0.987)
  Pallas kernels: 98.1 us -> 96.9 us
    pallas_call x1, Pallas kernels: 95.6 us -> 94.4 us  [local(): pl.pallas_call(kernel, out_shape=outs, in_specs=[anywhere] * 8, out_specs...]
where the time goes in v4:
time: 97.8 us; the launch traced here: 97.7 us
  Pallas kernels  96.9 us (99%)
    pallas_call x1, Pallas kernels, local(): pl.pallas_call(kernel, out_shape=outs, in_specs=[anywhere] * 8, out_specs...  94.4 us
    pallas_call x1, Pallas kernels, local(): pl.pallas_call(keep, out_shape=outs, in_specs=[anywhere] * 3, out_specs=(...  2.5 us

profile of v4, /device:TPU:1, one launch (start us, length us, event | category | flops | bytes accessed | tf_op | source)
XLA Modules:
  0.0 97.7 jit_solution(3389985640862041544)
XLA Ops:
  0.6 94.4 %shard_map.103 = (f32[64,4096]{1,0:T(8,128)}, f32[64,1024]{1,0:T(8,128)}, f32[64,4096]{1,0:T(8,128)}) custom-call(bf16[1024,4096]{1,0:T(8,128)(2,1)} %m_hbm.1, bf16[64,4096]{1,0:T(8,128)(2,1)} %cp_hbm.1, bf16[64,4096]{1,0:T(8,128)(2,1)} %ct_hbm.1, f32[64,1024]{1,0:T(8,128)} %d0_hbm.1, f32[1,1024]{1,0:T(1,128)} %bitcast.5, s32[1,4096]{1,0:T(1,128)} %bitcast.4, ...), custom_call_target="tpu_custom_call" | custom-call | tf_op jit(solution)/shard_map/pallas_call | solution.py:581
  95.1 2.5 %shard_map.104 = (f32[64,4096]{1,0:T(8,128)}, f32[64,1024]{1,0:T(8,128)}, f32[64,4096]{1,0:T(8,128)}) custom-call(f32[64,4096]{1,0:T(8,128)} %get-tuple-element.6.a, f32[64,1024]{1,0:T(8,128)} %get-tuple-element.7.b, f32[64,4096]{1,0:T(8,128)} %get-tuple-element.8.c), custom_call_target="tpu_custom_call" | custom-call | tf_op jit(solution)/shard_map/pallas_call | solution.py:600

commit v5 on v4

--- a/solution.py
+++ b/solution.py
@@ -29,8 +29,8 @@
 
 def kernel(
     m_hbm, cp_hbm, ct_hbm, d0_hbm, right_hbm, code_hbm, numer_hbm, denom_hbm,
-    primal_out, dual_out, grad_out,
-    primal_ref, dual_ref, grad_ref, out_sem, m_ref, m_sem, cp_ref, ct_ref, d0_ref, right_ref, code_ref, numer_ref, denom_ref, in_sem,
+    primal_ref, dual_ref, grad_ref,
+    m_ref, m_sem, cp_ref, ct_ref, d0_ref, right_ref, code_ref, numer_ref, denom_ref, in_sem,
     tau_ref, sigma_ref, theta_ref, scale2_ref, low_ref, high_ref, sum_ref,
     dbf_ref, own_ref, t0_ref, t1_ref, red0_ref, sh0_ref, slope0_ref, sa1_ref, e_ref, z_ref,
     s1x, s1z, r1x, r1z, s2z, s2x, r2z, r2x, gather,
@@ -459,8 +459,6 @@
     primal_process = with_product(primal_step, slice(INST, 2 * INST), (3,))
     for qx, qz in far_pieces:
         primal_process(flip(x, qx), flip(zl, qz))
-    primal_copy = pltpu.make_async_copy(primal_ref, primal_out, out_sem.at[0])
-    primal_copy.start()
     rows_t[1, yc] = to_row(tau_ref[:, 0:1] * jnp.sum(sum_ref[...], axis=1, keepdims=True))
     far = far_primal(2, sends)
     end_sends = scatter_primal(3)
@@ -504,43 +502,23 @@
         gradient = tau_ref[...] * (slope_adj + slope0_ref[:, cols] * ahead)
         grad_ref[:, cols] = cp_ref[:, cols].astype(F32) * sum_ref[...] - gradient
 
-    grad_process = halves(last_step)
-    out_copies = []
-
-    def process(gx, gz):
-        grad_process(gx, gz)
-        cols = at(gx * SIDE + gz, CHUNK)
-        copy = pltpu.make_async_copy(grad_ref.at[:, cols], grad_out.at[:, cols], out_sem.at[2 + len(out_copies)])
-        copy.start()
-        out_copies.append(copy)
-
-    dual_copy = pltpu.make_async_copy(dual_ref, dual_out, out_sem.at[1])
-
     def dual_end():
         wait_all(dual_gathers)
         for i in range(TEAM):
             dual_ref[:, i * PIECE : (i + 1) * PIECE] = gd[i]
-        dual_copy.start()
-
-    gather_dual(later, process, dual_end)
-    primal_copy.wait()
-    dual_copy.wait()
-    wait_all(out_copies)
-
-
-def keep(a, b, c, out_a, out_b, out_c, hold_a, hold_b, hold_c, in_sem, out_sem):
-    ways = [(b, hold_b, out_b)]
+
+    gather_dual(later, halves(last_step), dual_end)
+
+
+def keep(a, b, c, out_a, out_b, out_c, sem):
+    ways = [(b, out_b)]
     for n in range(4):
         rows = pl.ds(n * 16, 16)
-        ways.append((a.at[rows], hold_a.at[rows], out_a.at[rows]))
-        ways.append((c.at[rows], hold_c.at[rows], out_c.at[rows]))
-    loads = [pltpu.make_async_copy(src, hold, in_sem.at[n]) for n, (src, hold, _) in enumerate(ways)]
-    stores = [pltpu.make_async_copy(hold, dst, out_sem.at[n]) for n, (_, hold, dst) in enumerate(ways)]
-    for copy in loads:
+        ways.append((a.at[rows], out_a.at[rows]))
+        ways.append((c.at[rows], out_c.at[rows]))
+    stores = [pltpu.make_async_copy(src, dst, sem.at[n]) for n, (src, dst) in enumerate(ways)]
+    for copy in stores:
         copy.start()
-    for load, store in zip(loads, stores):
-        load.wait()
-        store.start()
     for copy in stores:
         copy.wait()
 
@@ -549,9 +527,9 @@
     dma = pltpu.SemaphoreType.DMA
     v = pltpu.VMEM
     anywhere = pl.BlockSpec(memory_space=pl.ANY)
+    whole = pl.BlockSpec(memory_space=pltpu.VMEM)
     uses, rows = 4, 3
     scratch = [
-        v((INST, COLS), F32), v((INST, ROWS), F32), v((INST, COLS), F32), dma((2 + SIDE * SIDE,)),
         v((ROWS, COLS), BF16), dma((SIDE,)), v((INST, COLS), BF16), v((INST, COLS), BF16), v((INST, ROWS), F32),
         v((1, ROWS), F32), v((1, COLS), jnp.int32), v((3, INST), jnp.int32), v((3, INST), jnp.int32), dma((7,)),
         v((INST, LANES), F32), v((INST, LANES), F32), v((INST, LANES), F32), v((INST, LANES), F32),
@@ -580,13 +558,14 @@
     )
     results = pl.pallas_call(
         kernel,
-        out_shape=outs,
+        out_shape=(v((INST, COLS), F32), v((INST, ROWS), F32), v((INST, COLS), F32)),
         in_specs=[anywhere] * 8,
-        out_specs=(anywhere,) * 3,
+        out_specs=(whole,) * 3,
         scratch_shapes=scratch,
         compiler_params=pltpu.CompilerParams(
-            collective_id=0, has_side_effects=True, vmem_limit_bytes=63 * 2**20
+            collective_id=0, has_side_effects=True, vmem_limit_bytes=58 * 2**20
         ),
+        cost_estimate=pl.CostEstimate(flops=10**11, bytes_accessed=0, transcendentals=0),
     )(
         matrix,
         cost_pred,
@@ -600,10 +579,10 @@
     return pl.pallas_call(
         keep,
         out_shape=outs,
-        in_specs=[anywhere] * 3,
+        in_specs=[whole] * 3,
         out_specs=(anywhere,) * 3,
-        scratch_shapes=[v((INST, COLS), F32), v((INST, ROWS), F32), v((INST, COLS), F32), dma((9,)), dma((9,))],
-        compiler_params=pltpu.CompilerParams(vmem_limit_bytes=63 * 2**20),
+        scratch_shapes=[dma((9,))],
+        compiler_params=pltpu.CompilerParams(vmem_limit_bytes=16 * 2**20),
     )(*results)
 
 

time: 97.8 us -> 96 us (0.982)
  Pallas kernels: 96.9 us -> 95.1 us
    pallas_call x2, Pallas kernels: 96.9 us -> 95.1 us  [the longest x1 93.7 us: local(): pl.pallas_call(kernel, out_shape=(v((INST, COLS), F32), v((INST, ROWS), F...]
where the time goes in v5:
time: 96 us; the launch traced here: 95.9 us
  Pallas kernels  95.1 us (99%)
    pallas_call x1, Pallas kernels, local(): pl.pallas_call(kernel, out_shape=(v((INST, COLS), F32), v((INST, ROWS), F...  93.7 us

profile of v5, /device:TPU:1, one launch (start us, length us, event | category | flops | bytes accessed | tf_op | source)
XLA Modules:
  0.0 95.9 jit_solution(11696541358940417706)
XLA Ops:
  0.6 93.7 %shard_map.103 = (f32[64,4096]{1,0:T(8,128)S(1)}, f32[64,1024]{1,0:T(8,128)S(1)}, f32[64,4096]{1,0:T(8,128)S(1)}) custom-call(bf16[1024,4096]{1,0:T(8,128)(2,1)} %m_hbm.1, bf16[64,4096]{1,0:T(8,128)(2,1)} %cp_hbm.1, bf16[64,4096]{1,0:T(8,128)(2,1)} %ct_hbm.1, f32[64,1024]{1,0:T(8,128)} %d0_hbm.1, f32[1,1024]{1,0:T(1,128)} %bitcast.5, s32[1,4096]{1,0:T(1,128)} %bitcast.4, ...), custom_call_target="tpu_custom_call" | custom-call | flops 99999997952 | tf_op jit(solution)/shard_map/pallas_call | solution.py:559
  94.3 1.5 %shard_map.104 = (f32[64,4096]{1,0:T(8,128)}, f32[64,1024]{1,0:T(8,128)}, f32[64,4096]{1,0:T(8,128)}) custom-call(f32[64,4096]{1,0:T(8,128)S(1)} %get-tuple-element.6.a, f32[64,1024]{1,0:T(8,128)S(1)} %get-tuple-element.7.b, f32[64,4096]{1,0:T(8,128)S(1)} %get-tuple-element.8.c), custom_call_target="tpu_custom_call" | custom-call | tf_op jit(solution)/shard_map/pallas_call | solution.py:579

commit v6 on v5

--- a/solution.py
+++ b/solution.py
@@ -22,7 +22,7 @@
 TEAM = 8
 PIECE = ROWS // TEAM
 LANES = 128
-CUT_OUT = 96
+CUT_OUT = 80
 STACK = INST * CHUNK // LANES
 REST = STACK - CUT
 

time: 96 us -> 96 us (level)
  no operation moved by 1% of the time
where the time goes in v6:
time: 96 us
  Pallas kernels  95.2 us (99%)
    pallas_call x1, Pallas kernels, local(): pl.pallas_call(kernel, out_shape=(v((INST, COLS), F32), v((INST, ROWS), F...  93.7 us

profile of v6, /device:TPU:1, one launch (start us, length us, event | category | flops | bytes accessed | tf_op | source)
XLA Modules:
  0.0 96.0 jit_solution(14268439586953711900)
XLA Ops:
  0.6 93.7 %shard_map.103 = (f32[64,4096]{1,0:T(8,128)S(1)}, f32[64,1024]{1,0:T(8,128)S(1)}, f32[64,4096]{1,0:T(8,128)S(1)}) custom-call(bf16[1024,4096]{1,0:T(8,128)(2,1)} %m_hbm.1, bf16[64,4096]{1,0:T(8,128)(2,1)} %cp_hbm.1, bf16[64,4096]{1,0:T(8,128)(2,1)} %ct_hbm.1, f32[64,1024]{1,0:T(8,128)} %d0_hbm.1, f32[1,1024]{1,0:T(1,128)} %bitcast.5, s32[1,4096]{1,0:T(1,128)} %bitcast.4, ...), custom_call_target="tpu_custom_call" | custom-call | flops 99999997952 | tf_op jit(solution)/shard_map/pallas_call | solution.py:559
  94.3 1.5 %shard_map.104 = (f32[64,4096]{1,0:T(8,128)}, f32[64,1024]{1,0:T(8,128)}, f32[64,4096]{1,0:T(8,128)}) custom-call(f32[64,4096]{1,0:T(8,128)S(1)} %get-tuple-element.6.a, f32[64,1024]{1,0:T(8,128)S(1)} %get-tuple-element.7.b, f32[64,4096]{1,0:T(8,128)S(1)} %get-tuple-element.8.c), custom_call_target="tpu_custom_call" | custom-call | tf_op jit(solution)/shard_map/pallas_call | solution.py:579
